TPU v7x, 512 devices: a whole 4x8x8 slice. The times are simulated.
512 devices in a mesh: vocab: 32 (over x_hi, y, core), seq: 16 (over x_lo, z).
Axes of the slice: x: 4 (x_hi: 2, x_lo: 2; x = x_hi * 2 + x_lo), y: 8, z: 8, core: 2. Of those that a mesh axis runs over, the one named last changes fastest.
Arguments:
- hidden: bfloat16 [2048, 3584], P('seq', 'vocab'), may hold values from -64 to 64
- table: bfloat16 [128000, 3584], P(('vocab', 'seq')), may hold values from -2 to 2
- targets: int32 [2048], replicated, may hold values from 0 to 127999
- token_ids: int32 [2048], P('seq'), may hold values from 0 to 127999, as said below
- input_grad: bfloat16 [2048, 3584], P('seq'), may hold values from -6 to 6
Outputs:
- token_loss: float32 [2048], P('seq')
- table_grad: bfloat16 [128000, 3584], P(('vocab', 'seq'))
Inputs may be any that keep to these rules, and one draw needn't show every extreme that they name: `token_ids`: among the 128 tokens of one index of seq, at most 12 have ids in the 4000 table rows of one index of vocab, and at most 1 distinct ids lie in the 250 rows of one device.
All inputs are finite; a program needn't handle non-finite values.
Results may differ from a plain program's by a relative error of at most 0.006.
Values may be sent and summed in bfloat16 or wider, within the bound.
A program may use at most 128 MiB of HBM per device.

v0:
```python
import jax
import jax.numpy as jnp
from jax import lax
from jax.sharding import PartitionSpec as P

HOT = 8


def on_device(hidden, table, targets, token_ids, input_grad):
    vocab_count = lax.axis_size("vocab")
    seq_count = lax.axis_size("seq")
    vocab_index = lax.axis_index("vocab")
    seq_index = lax.axis_index("seq")
    rows_here = table.shape[0]
    width = table.shape[1]
    tok_here = hidden.shape[0]
    row_start = (vocab_index * seq_count + seq_index) * rows_here
    full_features = lax.all_gather(hidden, "vocab", axis=1, tiled=True)
    piece = lax.all_gather(full_features, "seq", axis=0, tiled=True)
    piece_logits = lax.dot_general(
        piece, table, (((1,), (1,)), ((), ())), preferred_element_type=jnp.float32
    )
    logits = piece_logits
    hidden_all, logits = (piece, logits)
    column_ids = lax.broadcasted_iota(jnp.int32, (1, rows_here), 1)
    local_target = targets - row_start
    target_hit = local_target[:, None] == column_ids
    local_pick = jnp.sum(jnp.where(target_hit, logits, 0.0), axis=1)
    local_top = jnp.max(logits, axis=1)
    top_all = lax.pmax(local_top, ("vocab", "seq"))
    local_total = jnp.sum(jnp.exp(logits - top_all[:, None]), axis=1)
    total_all, picked_all = lax.psum((local_total, local_pick), ("vocab", "seq"))
    probs = jnp.exp(logits - top_all[:, None]) / total_all[:, None]
    score_grad = (probs - target_hit.astype(jnp.float32)).astype(jnp.bfloat16)
    head_grad = lax.dot_general(
        score_grad, hidden_all, (((0,), (0,)), ((), ())), preferred_element_type=jnp.float32
    )
    loss_all = top_all + jnp.log(total_all) - picked_all
    token_loss = lax.dynamic_slice_in_dim(loss_all, seq_index * tok_here, tok_here)
    per_group = (tok_here - HOT + vocab_count - 1) // vocab_count
    capacity = HOT + per_group
    group_start = vocab_index * seq_count * rows_here
    relative = token_ids - group_start
    member = (relative >= 0) & (relative < seq_count * rows_here)
    member_rank = jnp.cumsum(member.astype(jnp.int32)) - 1
    slot_ids = lax.broadcasted_iota(jnp.int32, (capacity, 1), 0)
    select = (member_rank[None, :] == slot_ids) & member[None, :]
    token_index = lax.broadcasted_iota(jnp.int32, (1, tok_here), 1)
    positions = jnp.sum(jnp.where(select, token_index, 0), axis=1)
    occupied = jnp.any(select, axis=1)
    send_rows = jnp.where(occupied[:, None], input_grad[positions], jnp.zeros((), jnp.bfloat16))
    send_ids = jnp.where(occupied, token_ids[positions], -1)
    got_rows, got_ids = (
        lax.all_gather(send_rows, "seq", axis=0, tiled=True),
        lax.all_gather(send_ids, "seq", axis=0, tiled=True),
    )
    local_ids = got_ids - row_start
    inside = (local_ids >= 0) & (local_ids < rows_here)
    target_rows = jnp.where(inside, local_ids, rows_here)
    embed_grad = (
        jnp.zeros((rows_here, width), jnp.float32)
        .at[target_rows]
        .add(got_rows.astype(jnp.float32), mode="drop")
    )
    table_grad = (head_grad + embed_grad).astype(jnp.bfloat16)
    return (token_loss, table_grad)


def solution(mesh):
    in_specs = (P("seq", "vocab"), P(("vocab", "seq"), None), P(), P("seq"), P("seq", None))
    out_specs = (P("seq"), P(("vocab", "seq"), None))
    return jax.shard_map(
        on_device, mesh=mesh, in_specs=in_specs, out_specs=out_specs, check_vma=False
    )
```

profile of v0, /device:TPU:1, one launch (start us, length us, event | category | flops | bytes accessed | tf_op | source)
XLA Modules:
  0.0 509.1 jit_solution(17139686175181942527)
XLA Ops:
  7.2 0.0 copy-start
  7.2 0.0 copy-start.1
  7.2 0.0 copy-start.2
  7.2 0.0 all-gather.6.cloned.1.call-start
  7.3 0.8 convert_bitcast_fusion
  8.0 0.1 copy.10
  8.1 0.2 reduce-window.8
  8.3 0.1 add_reduce_fusion
  8.4 0.1 fusion.6
  8.5 0.1 select_reduce_fusion.1
  8.7 2.0 gather_fusion.1
  10.7 0.7 select_bitcast_fusion
  11.4 0.0 all-gather.6.cloned.1.call-update
  11.4 0.0 all-gather.4.cloned.1.call-start
  11.5 49.8 %all_gather.12 = bf16[128,3584]{0,1:T(8,128)(2,1)} all-gather(bf16[128,112]{0,1:T(8,128)(2,1)} %param.5), channel_id=1, replica_groups=mesh['vocab'=32,'seq'=16] {'vocab'}, dimensions={1}, use_global_device_ids=true | all-gather | bytes 946176 | tf_op jit(solution)/shard_map/all_gather | solution.py:18
  61.3 0.0 all-gather.4.cloned.1.call-update
  61.3 0.0 copy-done.1
  61.3 0.7 gather_fusion
  62.0 1.3 dynamic-slice
  63.9 0.1 select_dynamic-update-slice_fusion
  64.0 18.4 %all-reduce = s32[192]{0:T(256)S(1)} all-reduce(s32[192]{0:T(256)S(1)} %select_dynamic-update-slice_fusion), channel_id=1, replica_groups=mesh['vocab'=32,'seq'=16] {'seq'}, use_global_device_ids=true, to_apply=%add | all-reduce | flops 192 | bytes 1536
  82.4 0.2 all-gather.6.cloned.1.call-done
  82.6 3.5 reshape.82
  86.1 183.3 %all-gather.4.cloned.1.call-done = bf16[2048,3584]{0,1:T(8,128)(2,1)} async-done(((bf16[128,3584]{0,1:T(8,128)(2,1)}), bf16[2048,3584]{0,1:T(8,128)(2,1)}) %all-gather.4.cloned.1.call-update) | async-done | bytes 14680080 | tf_op jit(solution)/shard_map/all_gather | solution.py:19
  269.4 8.7 %fusion.8 = (f32[2048]{0:T(1024)S(1)}, f32[2048,250]{0,1:T(8,128)}) fusion(bf16[2048,3584]{0,1:T(8,128)(2,1)} %all-gather.4.cloned.1.call-done, bf16[250,3584]{1,0:T(8,128)(2,1)S(1)} %copy-done), kind=kOutput, calls=%fused_computation.30 | convolution fusion | flops 3670525952 | bytes 18528256 | tf_op jit(solution)/shard_map/dot_general | solution.py:20
  278.1 102.5 %pmax.7 = f32[2048]{0:T(1024)S(1)} all-reduce(f32[2048]{0:T(1024)S(1)} %get-tuple-element.8), channel_id=1, replica_groups=mesh['vocab'=32,'seq'=16] {'vocab','seq'}, use_global_device_ids=true, to_apply=%region_1.2 | all-reduce | flops 2048 | bytes 16384 | tf_op jit(solution)/shard_map/pmax | solution.py:30
  380.6 2.1 fusion
  382.7 94.7 %all-reduce.1 = (f32[2048]{0:T(1024)S(1)}, f32[2048]{0:T(1024)S(1)}) all-reduce(f32[2048]{0:T(1024)S(1)} %get-tuple-element.3, f32[2048]{0:T(1024)S(1)} %get-tuple-element.2), channel_id=1, replica_groups=mesh['vocab'=32,'seq'=16] {'vocab','seq'}, use_global_device_ids=true, to_apply=%region_5.6 | all-reduce | flops 4096 | bytes 32768 | tf_op jit(solution)/shard_map/psum | solution.py:32
  477.4 11.7 %fusion.1 = f32[250,3584]{1,0:T(8,128)} fusion(bf16[2048,3584]{0,1:T(8,128)(2,1)} %all-gather.4.cloned.1.call-done, f32[2048,250]{0,1:T(8,128)} %get-tuple-element.9, f32[2048]{0:T(1024)S(1)} %get-tuple-element.5, s32[2048]{0:T(1024)S(1)} %broadcast_subtract_fusion, f32[2048]{0:T(1024)S(1)} %pmax.7), kind=kOutput, calls=%fused_computation.8 | convolution fusion | flops 3673088000 | bytes 20336640 | tf_op jit(solution)/shard_map/dot_general | solution.py:35
  489.0 9.1 %scatter_fusion = f32[250,3584]{1,0:T(8,128)} fusion(f32[250,3584]{1,0:T(8,128)} %fusion.1, s32[192]{0:T(256)S(1)} %compare_select_fusion, f32[192,3584]{1,0:T(8,128)} %reshape.82), kind=kCustom, calls=%fused_computation.2 | custom fusion | flops 688128 | bytes 8258304 | tf_op jit(solution)/shard_map/scatter-add | solution.py:63
  498.2 3.4 convert_element_type.16
  501.6 0.6 dynamic-slice_subtract_fusion
  (7 shorter events, 0.0 us)
Async XLA Ops:
  7.2 262.2 %copy-start = (bf16[250,3584]{1,0:T(8,128)(2,1)S(1)}, bf16[250,3584]{1,0:T(8,128)(2,1)}, u32[]{:S(2)}) copy-start(bf16[250,3584]{1,0:T(8,128)(2,1)} %param.6) | copy-start | bytes 5376004
  7.2 54.1 %copy-start.1 = (s32[128]{0:T(128)S(1)}, s32[128]{0:T(128)}, u32[]{:S(2)}) copy-start(s32[128]{0:T(128)} %param.8) | copy-start | bytes 1540
  7.2 75.2 %copy-start.2 = (s32[2048]{0:T(1024)S(1)}, s32[2048]{0:T(1024)}, u32[]{:S(2)}) copy-start(s32[2048]{0:T(1024)} %param.7) | copy-start | bytes 24580
  7.2 75.4 %all-gather.6.cloned.1.call-start = ((), (), s32[]{:S(2)}) async-start(), calls=%async_computation.1 | async-start | bytes 1949696 | tf_op jit(solution)/shard_map/all_gather | solution.py:54
  11.4 257.9 %all-gather.4.cloned.1.call-start = ((), (), s32[]{:S(2)}) async-start(), calls=%async_computation | async-start | bytes 15597568 | tf_op jit(solution)/shard_map/all_gather | solution.py:19
Sparse Core Ops, SparseCore 0:
  11.6 71.0 all-gather.5
  84.6 184.7 all-gather.3
where the time goes:
time: 510 us; the launch traced here: 509 us
  blocking collectives  265 us (52%)
  waiting for transfers between devices  184 us (36%)
  matrix products  20.4 us (4%)
  other arithmetic  17.4 us (3%)
  between operations  14.8 us (3%)
  local copies, waits for them, and re-layouts  7.57 us (1%)
    all_gather x1, waiting for transfers between devices, on_device(): piece = lax.all_gather(full_features, 'seq', axis=0, tiled=True)  183 us
    pmax x1, blocking collectives, on_device(): top_all = lax.pmax(local_top, ('vocab', 'seq'))  102 us
    psum x1, blocking collectives, on_device(): lax.psum((local_total, local_pick), ('vocab', 'seq'))  94.7 us
    all_gather x1, blocking collectives, on_device(): full_features = lax.all_gather(hidden, 'vocab', axis=1, tiled=True)  49.8 us
    unnamed x1, blocking collectives  18.4 us
    dot_general x1, matrix products, on_device(): lax.dot_general(score_grad, hidden_all, (((0,), (0,)), ((), ())), preferr...  11.7 us
  transfers between devices with their start and end apart: 2, of which 2 were waited for; matrix products, arithmetic and copies ran while one was open for 1% of the time, Pallas kernels for 0%

commit v1 on v0

v1 whole, which is shorter than its diff:
```python
import heapq
import itertools

import jax
import jax.numpy as jnp
from jax import lax
from jax.experimental import pallas as pl
from jax.experimental.pallas import tpu as pltpu
from jax.sharding import PartitionSpec as P

MESH = pl.DeviceIdType.MESH
F32 = jnp.float32
BF16 = jnp.bfloat16

D = 3584
TOK = 128
FEAT = 112
ROWS = 250
SEQ = 16
VOC = 32
HALF = D // 2
ROW_A, ROW_B, ROW_C = (0, 32), (32, 32), (64, 48)
EXTRA = D + 128


def plan_messages():
    messages = {}

    def put(key, size, axis, hops, deps):
        messages[key] = dict(size=size, axis=axis, hops=hops, deps=list(deps))

    def ring(name, unit, axis, size, length, deps, flip):
        far = (length // 2, length // 2 - 1)
        for step, most in zip((1, -1), far[::-1] if flip else far):
            for dist in range(1, most + 1):
                put((name, unit, step, dist), size, axis, 1, deps if dist == 1 else [(name, unit, step, dist - 1)])

    def item(name, unit, rel, length, flip):
        rel %= length
        back = length // 2 if flip else length // 2 - 1
        if rel == 0:
            return []
        return [(name, unit, -1, rel)] if rel <= back else [(name, unit, 1, length - rel)]

    a, b, c = ROW_A[1], ROW_B[1], ROW_C[1]
    for rel in (1, -1, 2, -2, 3, -3, 4):
        put(("CQ", 0, 1 if rel > 0 else -1, abs(rel)), c, "q", abs(rel), [])
    for rel in (1, -1, 2):
        put(("X1", 0, 1 if rel > 0 else -1, abs(rel)), a + b, "x", abs(rel), [])
    all_q = [key for key in messages if key[0] == "CQ"]
    all_x = [key for key in messages if key[0] == "X1"]
    ring("CP", 0, "p", 8 * c, 8, all_q, False)
    for rel in range(8):
        ring("CX", rel, "x", 8 * c, 4, all_q + item("CP", 0, rel, 8, False), rel % 2 == 1)
    ring("AQ", 0, "q", 4 * a, 8, all_x, False)
    ring("BP", 0, "p", 4 * b, 8, all_x, True)
    pair = {0: (1, -1), 1: (1, 2, 3), 3: (-1, -2, -3), 2: (2, 3, 4, 5, 6)}
    for name, axis, source, flip, rows in (("AP", "p", "AQ", False, a), ("BQ", "q", "BP", True, b)):
        for unit in range(4):
            deps = all_x + [key for rel in pair[unit] for key in item(source, 0, rel, 8, flip)]
            ring(name, unit, axis, 8 * rows, 8, deps, unit % 2 == 1)
    return messages


def plan_order(messages):
    turned = {"x": "x", "p": "q", "q": "p"}
    counter = itertools.count()
    link, issue, events = {}, [0.0, 0.0], []
    arrival = [{}, {}]
    waits = [{key: set(m["deps"]) for key, m in messages.items()} for _ in range(2)]
    after = {}
    for key, m in messages.items():
        for dep in m["deps"]:
            after.setdefault(dep, []).append(key)

    def start(core, key, now):
        m = messages[key]
        issue[core] = now = max(now, issue[core]) + 0.05
        lane = (turned[m["axis"]] if core else m["axis"], key[2])
        link[lane] = max(now, link.get(lane, 0.0)) + m["size"] * 256 * m["hops"] / 1e5
        heapq.heappush(events, (link[lane] + 1.0 + 0.3 * (m["hops"] - 1), next(counter), core, key))

    for core in range(2):
        for key, m in messages.items():
            if not m["deps"]:
                start(core, key, 0.0)
    while events:
        now, _, core, key = heapq.heappop(events)
        arrival[core][key] = now
        for later in after.get(key, []):
            waits[core][later].discard(key)
            if not waits[core][later]:
                start(core, later, now)
    return sorted(messages, key=lambda key: arrival[0][key] + arrival[1][key])


MESSAGES = plan_messages()
ORDER = plan_order(MESSAGES)
RECV = {key: i for i, key in enumerate(MESSAGES)}
PHASES = ("X1", "CQ", "CP", "CX", "AQ", "BP", "AP", "BQ")


def gather_kernel(
    hidden_ref, ids_hbm, input_grad_ref, table_ref, targets_ref,
    g, emb_rows, emb_hot, table_v, targets_v,
    ids_ref, grad_v, emb_out, emb_in,
    recv_sem, send_sem, core_sem, emb_sem, local_sem,
):
    v, s = lax.axis_index("vocab"), lax.axis_index("seq")
    c = lax.rem(v, 2)
    y = lax.rem(lax.div(v, 2), 8)
    z = lax.rem(s, 8)
    x = 2 * lax.div(v, 16) + lax.div(s, 8)
    p = z + c * (y - z)
    q = y + c * (z - y)

    def device(x_at, p_at, q_at):
        z_at = p_at + c * (q_at - p_at)
        y_at = q_at + c * (p_at - q_at)
        return (lax.div(x_at, 2) * 16 + y_at * 2 + c, lax.rem(x_at, 2) * 8 + z_at)

    def turn(at, by, length):
        return lax.rem(at + (by + length), length) if by else at

    sibling = (v + 1 - 2 * c, s)
    mine = g.at[c]
    other = g.at[1 - c]

    own_copy = pltpu.make_async_copy(hidden_ref, mine.at[x, p, q], local_sem.at[0])
    own_copy.start()
    ids_copy = pltpu.make_async_copy(ids_hbm, ids_ref, local_sem.at[1])
    ids_copy.start()
    grad_copy = pltpu.make_async_copy(input_grad_ref, grad_v, local_sem.at[2])
    grad_copy.start()
    targets_copy = pltpu.make_async_copy(targets_ref, targets_v, local_sem.at[3])
    targets_copy.start()
    table_copy = pltpu.make_async_copy(table_ref, table_v, local_sem.at[4])
    table_copy.start()

    partners = [device(turn(x, d, 4), p, q) for d in (1, -1, 2)]
    partners += [device(x, turn(p, d, 8), q) for d in (1, -1)]
    partners += [device(x, p, turn(q, d, 8)) for d in (1, -1, 2, -2, 3, -3, 4)]
    partners += [sibling]
    barrier = pltpu.get_barrier_semaphore()
    for partner in partners:
        pl.semaphore_signal(barrier, inc=1, device_id=partner, device_id_type=MESH)
    pl.semaphore_wait(barrier, len(partners))
    own_copy.wait()

    def rows(part_rows):
        return pl.ds(part_rows[0], part_rows[1])

    def block(name, unit, shift):
        if name == "X1":
            return mine.at[turn(x, shift, 4), p, q, pl.ds(ROW_A[0], ROW_A[1] + ROW_B[1])]
        if name == "CQ":
            return mine.at[x, p, turn(q, shift, 8), rows(ROW_C)]
        if name == "CP":
            return mine.at[x, turn(p, shift, 8), :, rows(ROW_C)]
        if name == "CX":
            return mine.at[turn(x, shift, 4), turn(p, unit, 8), :, rows(ROW_C)]
        if name == "AQ":
            return mine.at[:, p, turn(q, shift, 8), rows(ROW_A)]
        if name == "BP":
            return mine.at[:, turn(p, shift, 8), q, rows(ROW_B)]
        if name == "AP":
            pair = 2 * turn(lax.div(q, 2), unit, 4)
            return mine.at[:, turn(p, shift, 8), pl.ds(pair, 2), rows(ROW_A)]
        pair = 2 * turn(lax.div(p, 2), unit, 4)
        return mine.at[:, pl.ds(pair, 2), turn(q, shift, 8), rows(ROW_B)]

    def message(key):
        name, unit, step, dist = key
        m = MESSAGES[key]
        by = step * m["hops"]
        target = {
            "x": lambda: device(turn(x, by, 4), p, q),
            "p": lambda: device(x, turn(p, by, 8), q),
            "q": lambda: device(x, p, turn(q, by, 8)),
        }[m["axis"]]()
        data = block(name, unit, -step * (dist - m["hops"]))
        return pltpu.make_async_remote_copy(
            src_ref=data, dst_ref=data, send_sem=send_sem.at[PHASES.index(name)], recv_sem=recv_sem.at[RECV[key]],
            device_id=target, device_id_type=MESH,
        )

    def wait_message(key):
        name, unit, step, dist = key
        data = block(name, unit, -step * dist)
        pltpu.make_async_copy(data, data, recv_sem.at[RECV[key]]).wait()

    def to_sibling(data):
        pltpu.make_async_remote_copy(
            src_ref=data, dst_ref=data, send_sem=core_sem.at[0], recv_sem=core_sem.at[1],
            device_id=sibling, device_id_type=MESH,
        ).start()

    passes = []
    by_phase = lambda *names: [key for key in MESSAGES if key[0] in names]
    passes.append((by_phase("X1", "AQ"), lambda: mine.at[:, p, :, rows(ROW_A)]))
    passes.append((by_phase("X1", "BP"), lambda: mine.at[:, :, q, rows(ROW_B)]))
    passes.append((by_phase("CQ"), lambda: mine.at[x, p, :, rows(ROW_C)]))
    for rel in range(1, 8):
        def origin(name, unit_keys, rel=rel):
            return [k for k in by_phase(name) if (-k[2] * k[3]) % 8 == rel]
        passes.append((origin("AP", None), lambda rel=rel: mine.at[:, turn(p, rel, 8), :, rows(ROW_A)]))
        passes.append((origin("BQ", None), lambda rel=rel: mine.at[:, :, turn(q, rel, 8), rows(ROW_B)]))
    for key in by_phase("CP", "CX"):
        passes.append(([key], lambda key=key: block(key[0], key[1], -key[2] * key[3])))

    done = set()
    sent = set()
    passed = set()

    def send_ready():
        for key, m in MESSAGES.items():
            if key not in sent and all(dep in done for dep in m["deps"]):
                sent.add(key)
                message(key).start()
        for i, (deps, data) in enumerate(passes):
            if i not in passed and all(dep in done for dep in deps):
                passed.add(i)
                to_sibling(data())

    def embed_rows():
        ids_copy.wait()
        grad_copy.wait()
        first = lax.broadcasted_iota(jnp.int32, (SEQ, TOK), 0) * ROWS + v * (SEQ * ROWS)
        local = ids_ref[...] - first
        inside = (local >= 0) & (local < ROWS)
        total = jnp.dot(inside.astype(F32).astype(BF16), grad_v[...], preferred_element_type=F32)
        local_id = jnp.max(jnp.where(inside, local, -1).astype(F32), axis=1, keepdims=True)
        tail = jnp.broadcast_to(local_id, (SEQ, 128))
        for j in range(SEQ):
            emb_out[j, :, 0:D] = total[j : j + 1, :]
            emb_out[j, :, D:EXTRA] = tail[j : j + 1, :]
        emb_in[s] = emb_out[s]

        def send(r, carry):
            j = lax.rem(s + r, SEQ)
            pltpu.make_async_remote_copy(
                src_ref=emb_out.at[j], dst_ref=emb_in.at[s], send_sem=emb_sem.at[0], recv_sem=emb_sem.at[1],
                device_id=(v, j), device_id_type=MESH,
            ).start()
            return carry

        lax.fori_loop(1, SEQ, send, 0)

    send_ready()
    embedded = False
    needed = set(by_phase("X1", "AQ", "BP"))
    for key in ORDER:
        wait_message(key)
        done.add(key)
        send_ready()
        if not embedded and needed <= done:
            embedded = True
            embed_rows()

    def wait_bytes(data, sem):
        pltpu.make_async_copy(data, data, sem).wait()

    wait_bytes(emb_in.at[pl.ds(0, SEQ - 1)], emb_sem.at[1])
    lane_ids = lax.broadcasted_iota(jnp.int32, (1, ROWS), 1).astype(F32)
    for j in range(SEQ):
        emb_rows[j : j + 1, :] = emb_in[j, :, 0:D]
        emb_hot[j : j + 1, :] = (lane_ids == emb_in[j, :, D : D + 1]).astype(F32)

    targets_copy.wait()
    table_copy.wait()
    wait_bytes(mine.at[0:3, p, q, pl.ds(0, 64)], send_sem.at[0])
    wait_bytes(mine.at[x, p, 0:7, rows(ROW_C)], send_sem.at[1])
    wait_bytes(mine.at[x, 0:7, :, rows(ROW_C)], send_sem.at[2])
    wait_bytes(mine.at[0:3, :, :, rows(ROW_C)], send_sem.at[3])
    wait_bytes(mine.at[:, p, 0:7, rows(ROW_A)], send_sem.at[4])
    wait_bytes(mine.at[:, 0:7, q, rows(ROW_B)], send_sem.at[5])
    wait_bytes(mine.at[:, 0:7, :, rows(ROW_A)], send_sem.at[6])
    wait_bytes(mine.at[:, :, 0:7, rows(ROW_B)], send_sem.at[7])
    wait_bytes(emb_out.at[pl.ds(0, SEQ - 1)], emb_sem.at[0])
    wait_bytes(mine, core_sem.at[0])
    wait_bytes(other, core_sem.at[1])


def hit_of(targets_ref, block_index):
    row_start = (lax.axis_index("vocab") * SEQ + lax.axis_index("seq")) * ROWS
    row_ids = lax.broadcasted_iota(jnp.int32, (ROWS, TOK), 0)
    return (targets_ref[pl.ds(block_index, 1), :] - row_start) == row_ids


def logits_kernel(g, table_ref, targets_ref, logit, stat):
    def step(z_at, carry):
        columns = []
        for xl in range(2):
            halves = []
            for xh in range(2):
                even = g[0, 2 * xh + xl, z_at]
                odd = g[1, 2 * xh + xl, :, z_at]
                halves.append(jnp.stack([even, odd], axis=1).reshape(HALF, TOK))
            columns.append(jnp.concatenate(halves, axis=0))
        both = jnp.dot(table_ref[...], jnp.concatenate(columns, axis=1), preferred_element_type=F32)
        for xl in range(2):
            block_index = xl * 8 + z_at
            values = both[:, xl * TOK : (xl + 1) * TOK]
            logit[block_index] = values
            most = jnp.max(values, axis=0, keepdims=True)
            stat[block_index, 0:1, :] = most
            stat[block_index, 1:2, :] = jnp.sum(jnp.exp(values - most), axis=0, keepdims=True)
            hit = hit_of(targets_ref, block_index)
            stat[block_index, 2:3, :] = jnp.sum(jnp.where(hit, values, 0.0), axis=0, keepdims=True)
        return carry

    lax.fori_loop(0, 8, step, 0)


def combine(ref):
    most = jnp.max(ref[:, 0, :], axis=0, keepdims=True)
    total = jnp.sum(ref[:, 1, :] * jnp.exp(ref[:, 0, :] - most), axis=0, keepdims=True)
    return most, total, jnp.sum(ref[:, 2, :], axis=0, keepdims=True)


def stats_kernel(stat, top_in, loss_ref, stat_in, part, part_in, top, stat_sem, part_sem, top_sem):
    v, s = lax.axis_index("vocab"), lax.axis_index("seq")
    barrier = pltpu.get_barrier_semaphore()

    def greet(r, carry):
        pl.semaphore_signal(barrier, inc=1, device_id=(v, lax.rem(s + r, SEQ)), device_id_type=MESH)
        return carry

    def greet_vocab(r, carry):
        pl.semaphore_signal(barrier, inc=1, device_id=(lax.rem(v + r, VOC), s), device_id_type=MESH)
        return carry

    lax.fori_loop(1, SEQ, greet, 0)
    lax.fori_loop(1, VOC, greet_vocab, 0)
    pl.semaphore_wait(barrier, SEQ + VOC - 2)

    def wait_bytes(data, sem):
        pltpu.make_async_copy(data, data, sem).wait()

    def scatter(r, carry):
        j = lax.rem(s + r, SEQ)
        pltpu.make_async_remote_copy(
            src_ref=stat.at[j], dst_ref=stat_in.at[s], send_sem=stat_sem.at[0], recv_sem=stat_sem.at[1],
            device_id=(v, j), device_id_type=MESH,
        ).start()
        return carry

    lax.fori_loop(1, SEQ, scatter, 0)
    stat_in[s] = stat[s]
    wait_bytes(stat_in.at[pl.ds(0, SEQ - 1)], stat_sem.at[1])
    most, total, picked = combine(stat_in)
    part[0:1, :] = most
    part[1:2, :] = total
    part[2:3, :] = picked

    def exchange(r, carry):
        j = lax.rem(v + r, VOC)
        pltpu.make_async_remote_copy(
            src_ref=part, dst_ref=part_in.at[v], send_sem=part_sem.at[0], recv_sem=part_sem.at[1],
            device_id=(j, s), device_id_type=MESH,
        ).start()
        return carry

    lax.fori_loop(1, VOC, exchange, 0)
    part_in[v] = part[...]
    wait_bytes(part_in.at[pl.ds(0, VOC - 1)], part_sem.at[1])
    most, total, picked = combine(part_in)
    top[0:1, :] = most
    top[1:2, :] = 1.0 / total

    def spread(r, carry):
        j = lax.rem(s + r, SEQ)
        pltpu.make_async_remote_copy(
            src_ref=top, dst_ref=top_in.at[s], send_sem=top_sem.at[0], recv_sem=top_sem.at[1],
            device_id=(v, j), device_id_type=MESH,
        ).start()
        return carry

    lax.fori_loop(1, SEQ, spread, 0)
    top_in[s] = top[...]
    loss_ref[...] = most + jnp.log(total) - picked
    wait_bytes(top_in.at[pl.ds(0, SEQ - 1)], top_sem.at[1])
    wait_bytes(stat_in.at[pl.ds(0, SEQ - 1)], stat_sem.at[0])
    wait_bytes(part_in.at[pl.ds(0, VOC - 1)], part_sem.at[0])
    wait_bytes(top_in.at[pl.ds(0, SEQ - 1)], top_sem.at[0])


def head_kernel(g, logit, top_in, targets_ref, emb_rows, emb_hot, loss_in, loss_ref, out_ref, score, out_v, out_sem):
    loss_ref[...] = loss_in[...]

    def score_step(block_index, carry):
        probs = jnp.exp(logit[block_index] - top_in[block_index, 0:1, :]) * top_in[block_index, 1:2, :]
        value = probs - hit_of(targets_ref, block_index).astype(F32)
        score[:, pl.ds(pl.multiple_of(block_index * TOK, TOK), TOK)] = value.astype(BF16)
        return carry

    lax.fori_loop(0, SEQ, score_step, 0)
    hot = emb_hot[...].astype(BF16)
    hot = jnp.concatenate([hot, hot, hot], axis=0)
    width = D // 4

    def head_step(i, carry):
        xh, y_first = lax.div(i, 2), 4 * lax.rem(i, 2)
        columns = []
        for xl in range(2):
            for z_at in range(8):
                even = g[0, 2 * xh + xl, z_at, pl.ds(y_first, 4)]
                odd = g[1, 2 * xh + xl, pl.ds(y_first, 4), z_at]
                columns.append(jnp.stack([even, odd], axis=1).reshape(width, TOK))
        features = jnp.concatenate(columns, axis=1)
        at = pl.ds(pl.multiple_of(i * width, 128), width)
        total = lax.dot_general(score[...], features, (((1,), (1,)), ((), ())), preferred_element_type=F32)
        rest = emb_rows[:, at]
        high = rest.astype(BF16)
        rest = rest - high.astype(F32)
        middle = rest.astype(BF16)
        low = (rest - middle.astype(F32)).astype(BF16)
        terms = jnp.concatenate([high, middle, low], axis=0)
        total += lax.dot_general(hot, terms, (((0,), (0,)), ((), ())), preferred_element_type=F32)
        out_v[:, at] = total.astype(BF16)
        pltpu.make_async_copy(out_v.at[:, at], out_ref.at[:, at], out_sem).start()
        return carry

    lax.fori_loop(0, 4, head_step, 0)
    pltpu.make_async_copy(out_v, out_ref, out_sem).wait()


def on_device(hidden, table, targets, token_ids, input_grad):
    any_space = pl.BlockSpec(memory_space=pl.ANY)
    vmem = pl.BlockSpec(memory_space=pltpu.VMEM)
    dma = pltpu.SemaphoreType.DMA
    targets = targets.reshape(SEQ, TOK)
    g, emb_rows, emb_hot, table, targets = pl.pallas_call(
        gather_kernel,
        out_shape=(
            pltpu.VMEM((2, 4, 8, 8, FEAT, TOK), BF16),
            pltpu.VMEM((SEQ, D), F32),
            pltpu.VMEM((SEQ, ROWS), F32),
            pltpu.VMEM((ROWS, D), BF16),
            pltpu.VMEM((SEQ, TOK), jnp.int32),
        ),
        in_specs=[any_space] * 5,
        out_specs=(vmem,) * 5,
        scratch_shapes=[
            pltpu.VMEM((1, TOK), jnp.int32),
            pltpu.VMEM((TOK, D), BF16),
            pltpu.VMEM((SEQ, 1, EXTRA), F32),
            pltpu.VMEM((SEQ, 1, EXTRA), F32),
            dma((len(MESSAGES),)),
            dma((len(PHASES),)),
            dma((2,)),
            dma((2,)),
            dma((5,)),
        ],
        compiler_params=pltpu.CompilerParams(collective_id=0, has_side_effects=True, vmem_limit_bytes=47 * 2**20),
        name="gather",
    )(hidden.T, token_ids.reshape(1, TOK), input_grad, table, targets)
    logit, stat = pl.pallas_call(
        logits_kernel,
        out_shape=(pltpu.VMEM((SEQ, ROWS, TOK), F32), pltpu.VMEM((SEQ, 8, TOK), F32)),
        in_specs=[vmem, vmem, vmem],
        out_specs=(vmem, vmem),
        compiler_params=pltpu.CompilerParams(vmem_limit_bytes=24 * 2**20),
        cost_estimate=pl.CostEstimate(flops=2 * 2048 * ROWS * D, bytes_accessed=2**21, transcendentals=2048 * ROWS),
        name="logits",
    )(g, table, targets)
    top_in, loss = pl.pallas_call(
        stats_kernel,
        out_shape=(pltpu.VMEM((SEQ, 8, TOK), F32), pltpu.VMEM((1, TOK), F32)),
        in_specs=[vmem],
        out_specs=(vmem, vmem),
        scratch_shapes=[
            pltpu.VMEM((SEQ, 8, TOK), F32),
            pltpu.VMEM((8, TOK), F32),
            pltpu.VMEM((VOC, 8, TOK), F32),
            pltpu.VMEM((8, TOK), F32),
            dma((2,)),
            dma((2,)),
            dma((2,)),
        ],
        compiler_params=pltpu.CompilerParams(collective_id=1, has_side_effects=True, vmem_limit_bytes=4 * 2**20),
        name="stats",
    )(stat)
    loss, table_grad = pl.pallas_call(
        head_kernel,
        out_shape=(jax.ShapeDtypeStruct((1, TOK), F32), jax.ShapeDtypeStruct((ROWS, D), BF16)),
        in_specs=[vmem] * 7,
        out_specs=(vmem, any_space),
        scratch_shapes=[pltpu.VMEM((ROWS, SEQ * TOK), BF16), pltpu.VMEM((ROWS, D), BF16), dma],
        compiler_params=pltpu.CompilerParams(vmem_limit_bytes=24 * 2**20),
        cost_estimate=pl.CostEstimate(flops=2 * 2048 * ROWS * D, bytes_accessed=2**21, transcendentals=2048 * ROWS),
        name="head",
    )(g, logit, top_in, targets, emb_rows, emb_hot, loss)
    return loss.reshape(TOK), table_grad


def solution(mesh):
    in_specs = (P("seq", "vocab"), P(("vocab", "seq"), None), P(), P("seq"), P("seq", None))
    out_specs = (P("seq"), P(("vocab", "seq"), None))
    return jax.shard_map(
        on_device, mesh=mesh, in_specs=in_specs, out_specs=out_specs, check_vma=False
    )
```

time: 510 us -> 99 us (0.19)
  blocking collectives: 265 us -> 0 us
  waiting for transfers between devices: 184 us -> 0 us
  Pallas kernels: 0 us -> 98.2 us
  matrix products: 20.4 us -> 0 us
  other arithmetic: 17.4 us -> 0 us
  between operations: 14.8 us -> 0.65 us
  local copies, waits for them, and re-layouts: 7.57 us -> 0 us
    all_gather x2 -> x0, waiting for transfers between devices: 183 us -> none  [the longest x1 183 us: on_device(): piece = lax.all_gather(full_features, 'seq', axis=0, tiled=True)]
    pmax x1 -> x0, blocking collectives: 102 us -> none  [on_device(): top_all = lax.pmax(local_top, ('vocab', 'seq'))]
    pallas_call x0 -> x4, Pallas kernels: none -> 98.2 us  [the longest x1 63.1 us: on_device(): pl.pallas_call(gather_kernel, out_shape=(pltpu.VMEM((2, 4, 8, 8, FEAT, TO...]
    psum x1 -> x0, blocking collectives: 94.7 us -> none  [on_device(): lax.psum((local_total, local_pick), ('vocab', 'seq'))]
    all_gather x1 -> x0, blocking collectives: 49.8 us -> none  [on_device(): full_features = lax.all_gather(hidden, 'vocab', axis=1, tiled=True)]
    dot_general x2 -> x0, matrix products: 20.4 us -> none  [the longest x1 11.7 us: on_device(): lax.dot_general(score_grad, hidden_all, (((0,), (0,)), ((), ())), preferr...]
    unnamed x1 -> x0, blocking collectives: 18.4 us -> none
    scatter-add x1 -> x0, other arithmetic: 9.14 us -> none  [on_device(): embed_grad = jnp.zeros((rows_here, width), jnp.float32).at[target_rows].a...]
  transfers between devices with their start and end apart: 2 -> 0, of which waited for: 2 -> 0; matrix products, arithmetic and copies ran while one was open for 1% -> 0% of each run, Pallas kernels for 0% -> 0%
where the time goes in v1:
time: 99 us; the launch traced here: 98.8 us
  Pallas kernels  98.2 us (99%)
    pallas_call x1, Pallas kernels, on_device(): pl.pallas_call(gather_kernel, out_shape=(pltpu.VMEM((2, 4, 8, 8, FEAT, TO...  63.1 us
    pallas_call x1, Pallas kernels, on_device(): pl.pallas_call(stats_kernel, out_shape=(pltpu.VMEM((SEQ, 8, TOK), F32), p...  21.6 us
    pallas_call x1, Pallas kernels, on_device(): pl.pallas_call(head_kernel, out_shape=(jax.ShapeDtypeStruct((1, TOK), F32...  7.65 us
    pallas_call x1, Pallas kernels, on_device(): pl.pallas_call(logits_kernel, out_shape=(pltpu.VMEM((SEQ, ROWS, TOK), F32...  5.79 us

profile of v1, /device:TPU:1, one launch (start us, length us, event | category | flops | bytes accessed | tf_op | source)
XLA Modules:
  0.0 98.8 jit_solution(817024484251560655)
XLA Ops:
  0.6 63.1 %gather.1 = (bf16[2,4,8,8,112,128]{5,4,3,2,1,0:T(8,128)(2,1)S(1)}, f32[16,3584]{1,0:T(8,128)S(1)}, f32[16,250]{1,0:T(8,128)S(1)}, bf16[250,3584]{1,0:T(8,128)(2,1)S(1)}, s32[16,128]{1,0:T(8,128)S(1)}) custom-call(bf16[112,128]{1,0:T(8,128)(2,1)} %bitcast.4, s32[1,128]{1,0:T(1,128)} %bitcast.6, bf16[128,3584]{1,0:T(8,128)(2,1)} %input_grad_ref.1, ...), custom_call_target="tpu_custom_call" | custom-call | tf_op jit(solution)/shard_map/gather/pallas_call | solution.py:433
  63.7 5.8 %logits.1 = (f32[16,250,128]{2,1,0:T(8,128)S(1)}, f32[16,8,128]{2,1,0:T(8,128)S(1)}) custom-call(bf16[2,4,8,8,112,128]{5,4,3,2,1,0:T(8,128)(2,1)S(1)} %get-tuple-element.13.g, bf16[250,3584]{1,0:T(8,128)(2,1)S(1)} %get-tuple-element.14.table_ref, s32[16,128]{1,0:T(8,128)S(1)} %get-tuple-element.15.targets_ref), custom_call_target="tpu_custom_call" | custom-call | flops 3670016000 | bytes 2097152 | tf_op jit(solution)/shard_map/logits/pallas_call | solution.py:458
  69.5 21.6 %stats.1 = (f32[16,8,128]{2,1,0:T(8,128)S(1)}, f32[1,128]{1,0:T(1,128)S(1)}) custom-call(f32[16,8,128]{2,1,0:T(8,128)S(1)} %get-tuple-element.17.stat), custom_call_target="tpu_custom_call" | custom-call | tf_op jit(solution)/shard_map/stats/pallas_call | solution.py:467
  91.2 7.6 %head.1 = (f32[1,128]{1,0:T(1,128)}, bf16[250,3584]{1,0:T(8,128)(2,1)}) custom-call(bf16[2,4,8,8,112,128]{5,4,3,2,1,0:T(8,128)(2,1)S(1)} %get-tuple-element.13.g, f32[16,250,128]{2,1,0:T(8,128)S(1)} %get-tuple-element.16.logit, f32[16,8,128]{2,1,0:T(8,128)S(1)} %get-tuple-element.18.top_in, s32[16,128]{1,0:T(8,128)S(1)} %get-tuple-element.15.targets_ref, ...), custom_call_target="tpu_custom_call" | custom-call | flops 3670016000 | bytes 2097152 | tf_op jit(solution)/shard_map/head/pallas_call | solution.py:484

commit v2 on v0

v2 whole, which is shorter than its diff:
```python
import heapq
import itertools

import jax
import jax.numpy as jnp
from jax import lax
from jax.experimental import pallas as pl
from jax.experimental.pallas import tpu as pltpu
from jax.sharding import PartitionSpec as P

MESH = pl.DeviceIdType.MESH
F32 = jnp.float32
BF16 = jnp.bfloat16

D = 3584
TOK = 128
FEAT = 112
ROWS = 250
SEQ = 16
HALF = D // 2
EXTRA = D + 128
LEN_A, LEN_B, LEN_C = 32, 32, 48
GROUP = 4
PAIR = 1


def plan_messages():
    messages = {}

    def put(key, size, axis, hops, deps):
        messages[key] = dict(size=size * 256, axis=axis, hops=hops, deps=list(deps))

    def direct(name, axis, size, rels):
        for rel in rels:
            put((name, 0, 1 if rel > 0 else -1, abs(rel)), size, axis, abs(rel), [])

    def ring(name, unit, axis, size, length, deps, flip, stride=1):
        far = (length // 2, length // 2 - 1)
        for step, most in zip((1, -1), far[::-1] if flip else far):
            for dist in range(1, most + 1):
                hops = (dist - 1) % stride + 1
                put((name, unit, step, dist), size, axis, hops, deps if dist == hops else [(name, unit, step, dist - hops)])

    def item(name, rel, flip):
        rel %= 8
        back = 4 if flip else 3
        if rel == 0:
            return []
        return [(name, 0, -1, rel)] if rel <= back else [(name, 0, 1, 8 - rel)]

    def of(*names):
        return [key for key in messages if key[0] in names]

    whole = {
        1: {rel: (rel,) for rel in (0, 1, 7, 2, 6, 3, 5, 4)},
        2: {0: (1, -1), 1: (1, 2, 3), 3: (-1, -2, -3), 2: (2, 3, 4, 5, 6)},
        4: {0: (1, 2, 3, -1, -2, -3), 1: tuple(range(1, 8))},
    }
    direct("CQ", "q", LEN_C, (1, -1, 2, -2, 3, -3, 4))
    direct("XA", "x", LEN_A, (1, -1, 2))
    direct("XB", "x", LEN_B, (1, -1, 2))
    ring("CP", 0, "p", 8 * LEN_C, 8, of("CQ"), False)
    for unit, rels in whole[PAIR].items():
        deps = of("CQ") + [key for rel in rels for key in item("CP", rel, False)]
        ring("CX", unit, "x", PAIR * 8 * LEN_C, 4, deps, unit % 2 == 1)
    ring("AQ", 0, "q", 4 * LEN_A, 8, of("XA"), False, 2)
    ring("BP", 0, "p", 4 * LEN_B, 8, of("XB"), True, 2)
    for name, axis, first, source, flip, size in (("AP", "p", "XA", "AQ", False, LEN_A), ("BQ", "q", "XB", "BP", True, LEN_B)):
        for unit, rels in whole[GROUP].items():
            deps = of(first) + [key for rel in rels for key in item(source, rel, flip)]
            ring(name, unit, axis, 4 * GROUP * size, 8, deps, unit % 2 == 1)
    put(("SA", 0, 0, 0), 32 * LEN_A, "s", 1, of("XA", "AQ"))
    put(("SB", 0, 0, 0), 32 * LEN_B, "s", 1, of("XB", "BP"))
    put(("SC", 0, 0, 0), 64 * LEN_C, "s", 1, of("CQ", "CP"))
    for rel in range(1, 8):
        for name, source, size in (("SA", "AP", LEN_A), ("SB", "BQ", LEN_B)):
            put((name, rel, 0, 0), 32 * size, "s", 1, [k for k in of(source) if (-k[2] * k[3]) % 8 == rel])
    for key in of("CX"):
        put(("SC",) + key, PAIR * 8 * LEN_C, "s", 1, [key])
    return messages


def plan_order(messages):
    turned = {"x": "x", "p": "q", "q": "p", "s": "s"}
    counter = itertools.count()
    link, free, events = {}, [0.0, 0.0], []
    arrival = [{}, {}]
    waits = [{key: set(m["deps"]) for key, m in messages.items()} for _ in range(2)]
    after = {}
    for key, m in messages.items():
        for dep in m["deps"]:
            after.setdefault(dep, []).append(key)

    def start(core, key, now):
        m = messages[key]
        free[core] = now = max(now, free[core]) + 0.05
        lane = ("s", core) if m["axis"] == "s" else (turned[m["axis"]] if core else m["axis"], key[2])
        rate = 6e5 if m["axis"] == "s" else 8.5e4
        link[lane] = max(now, link.get(lane, 0.0)) + m["size"] * m["hops"] / rate
        heapq.heappush(events, (link[lane] + 3.0 + 0.5 * (m["hops"] - 1), next(counter), core, key))

    for core in range(2):
        for key, m in messages.items():
            if not m["deps"]:
                start(core, key, 0.0)
    while events:
        now, _, core, key = heapq.heappop(events)
        arrival[core][key] = now
        for later in after.get(key, []):
            waits[core][later].discard(key)
            if not waits[core][later]:
                start(core, later, now)
    here = [key for key, m in messages.items() if m["axis"] != "s"]
    return sorted(here, key=lambda key: arrival[0][key] + arrival[1][key])


MESSAGES = plan_messages()
ORDER = plan_order(MESSAGES)
RECV = {key: i for i, key in enumerate(ORDER)}
PHASES = ("XA", "XB", "CQ", "CP", "CX", "AQ", "BP", "AP", "BQ")


def wait_bytes(data, sem):
    pltpu.make_async_copy(data, data, sem).wait()


def gather_kernel(
    hidden_ref, ids_hbm, input_grad_ref, table_ref, targets_ref,
    part_a, part_b, part_c, emb_rows, emb_hot, table_v, targets_v,
    ids_ref, grad_v, emb_out, emb_in,
    recv_sem, send_sem, core_sem, emb_sem, local_sem,
):
    v, s = lax.axis_index("vocab"), lax.axis_index("seq")
    c = lax.rem(v, 2)
    y = lax.rem(lax.div(v, 2), 8)
    z = lax.rem(s, 8)
    x = 2 * lax.div(v, 16) + lax.div(s, 8)
    p = z + c * (y - z)
    q = y + c * (z - y)

    def device(x_at, p_at, q_at):
        z_at = p_at + c * (q_at - p_at)
        y_at = q_at + c * (p_at - q_at)
        return (lax.div(x_at, 2) * 16 + y_at * 2 + c, lax.rem(x_at, 2) * 8 + z_at)

    def turn(at, by, length):
        return lax.rem(at + (by + length), length) if by else at

    sibling = (v + 1 - 2 * c, s)
    a, b, cc = part_a.at[c], part_b.at[c], part_c.at[c]

    own = [
        pltpu.make_async_copy(hidden_ref.at[pl.ds(LEN_A + LEN_B, LEN_C)], cc.at[x, p, q], local_sem.at[0]),
        pltpu.make_async_copy(hidden_ref.at[pl.ds(0, LEN_A)], a.at[p, q, x], local_sem.at[1]),
        pltpu.make_async_copy(hidden_ref.at[pl.ds(LEN_A, LEN_B)], b.at[q, p, x], local_sem.at[2]),
    ]
    ids_copy = pltpu.make_async_copy(ids_hbm, ids_ref, local_sem.at[3])
    grad_copy = pltpu.make_async_copy(input_grad_ref, grad_v, local_sem.at[4])
    targets_copy = pltpu.make_async_copy(targets_ref, targets_v, local_sem.at[5])
    table_copy = pltpu.make_async_copy(table_ref, table_v, local_sem.at[6])
    for copy in own:
        copy.start()

    partners = [device(turn(x, d, 4), p, q) for d in (1, -1, 2)]
    partners += [device(x, turn(p, d, 8), q) for d in (1, -1, 2, -2)]
    partners += [device(x, p, turn(q, d, 8)) for d in (1, -1, 2, -2, 3, -3, 4)]
    partners += [sibling]
    barrier = pltpu.get_barrier_semaphore()
    for partner in partners:
        pl.semaphore_signal(barrier, inc=1, device_id=partner, device_id_type=MESH)
    for copy in (ids_copy, grad_copy, targets_copy, table_copy):
        copy.start()
    for copy in own:
        copy.wait()
    pl.semaphore_wait(barrier, len(partners))

    def group(at, unit, size):
        return pl.ds(size * turn(lax.div(at, size), unit, 8 // size), size)

    def block(key, shift):
        name, unit = key[0], key[1]
        if name == "XA":
            return a.at[p, q, turn(x, shift, 4)]
        if name == "XB":
            return b.at[q, p, turn(x, shift, 4)]
        if name == "CQ":
            return cc.at[x, p, turn(q, shift, 8)]
        if name == "CP":
            return cc.at[x, turn(p, shift, 8)]
        if name == "CX":
            return cc.at[turn(x, shift, 4), group(p, unit, PAIR)]
        if name == "AQ":
            return a.at[p, turn(q, shift, 8)]
        if name == "BP":
            return b.at[q, turn(p, shift, 8)]
        if name == "AP":
            return a.at[turn(p, shift, 8), group(q, unit, GROUP)]
        if name == "BQ":
            return b.at[turn(q, shift, 8), group(p, unit, GROUP)]
        if name == "SA":
            return a.at[turn(p, unit, 8)]
        if name == "SB":
            return b.at[turn(q, unit, 8)]
        return arrived(key[1:]) if unit else cc.at[x]

    def arrived(key):
        return block(key, -key[2] * key[3])

    def send(key):
        m = MESSAGES[key]
        if m["axis"] == "s":
            part = ("SA", "SB", "SC").index(key[0])
            data, target, sems = block(key, 0), sibling, (core_sem.at[0, part], core_sem.at[1, part])
        else:
            by = key[2] * m["hops"]
            data = block(key, -key[2] * (key[3] - m["hops"]))
            target = {
                "x": lambda: device(turn(x, by, 4), p, q),
                "p": lambda: device(x, turn(p, by, 8), q),
                "q": lambda: device(x, p, turn(q, by, 8)),
            }[m["axis"]]()
            sems = send_sem.at[PHASES.index(key[0])], recv_sem.at[RECV[key]]
        pltpu.make_async_remote_copy(
            src_ref=data, dst_ref=data, send_sem=sems[0], recv_sem=sems[1], device_id=target, device_id_type=MESH
        ).start()

    done, sent = set(), set()

    def send_ready():
        for key, m in MESSAGES.items():
            if key not in sent and all(dep in done for dep in m["deps"]):
                sent.add(key)
                send(key)

    def embed_rows():
        ids_copy.wait()
        grad_copy.wait()
        first = lax.broadcasted_iota(jnp.int32, (SEQ, TOK), 0) * ROWS + v * (SEQ * ROWS)
        local = ids_ref[...] - first
        inside = (local >= 0) & (local < ROWS)
        total = jnp.dot(inside.astype(F32).astype(BF16), grad_v[...], preferred_element_type=F32)
        local_id = jnp.max(jnp.where(inside, local, -1).astype(F32), axis=1, keepdims=True)
        tail = jnp.broadcast_to(local_id, (SEQ, 128))
        for j in range(SEQ):
            emb_out[j, :, 0:D] = total[j : j + 1, :]
            emb_out[j, :, D:EXTRA] = tail[j : j + 1, :]
        emb_in[s] = emb_out[s]

        def send_row(r, carry):
            j = lax.rem(s + r, SEQ)
            pltpu.make_async_remote_copy(
                src_ref=emb_out.at[j], dst_ref=emb_in.at[s], send_sem=emb_sem.at[0], recv_sem=emb_sem.at[1],
                device_id=(v, j), device_id_type=MESH,
            ).start()
            return carry

        lax.fori_loop(1, SEQ, send_row, 0)

    def embed_arrived():
        wait_bytes(emb_in.at[pl.ds(0, SEQ - 1)], emb_sem.at[1])
        lane_ids = lax.broadcasted_iota(jnp.int32, (1, ROWS), 1).astype(F32)
        for j in range(SEQ):
            emb_rows[j : j + 1, :] = emb_in[j, :, 0:D]
            emb_hot[j : j + 1, :] = (lane_ids == emb_in[j, :, D : D + 1]).astype(F32)

    send_ready()
    embedded = False
    needed = {key for key in MESSAGES if key[0] in ("XA", "XB", "AQ", "BP")}
    for key in ORDER:
        wait_bytes(arrived(key), recv_sem.at[RECV[key]])
        done.add(key)
        send_ready()
        if not embedded and needed <= done:
            embedded = True
            embed_rows()
        if len(done) == len(ORDER) * 4 // 5:
            embed_arrived()

    targets_copy.wait()
    table_copy.wait()
    wait_bytes(a.at[p, q, 0:3], send_sem.at[0])
    wait_bytes(b.at[q, p, 0:3], send_sem.at[1])
    wait_bytes(cc.at[x, p, 0:7], send_sem.at[2])
    wait_bytes(cc.at[x, 0:7], send_sem.at[3])
    wait_bytes(cc.at[0:3], send_sem.at[4])
    wait_bytes(a.at[p, 0:7], send_sem.at[5])
    wait_bytes(b.at[q, 0:7], send_sem.at[6])
    wait_bytes(a.at[0:7], send_sem.at[7])
    wait_bytes(b.at[0:7], send_sem.at[8])
    wait_bytes(emb_out.at[pl.ds(0, SEQ - 1)], emb_sem.at[0])
    for side in (0, 1):
        for i, data in enumerate((part_a, part_b, part_c)):
            wait_bytes(data.at[1 - c] if side else data.at[c], core_sem.at[side, i])


def hit_of(targets_ref, z_at):
    row_start = (lax.axis_index("vocab") * SEQ + lax.axis_index("seq")) * ROWS
    row_ids = lax.broadcasted_iota(jnp.int32, (ROWS, 2 * TOK), 0)
    both = jnp.concatenate([targets_ref[pl.ds(8 * xl + z_at, 1), :] for xl in range(2)], axis=1)
    return (both - row_start) == row_ids


def features_of(parts, xh, xl, z_at, ys):
    part_a, part_b, part_c = parts
    x = 2 * xh + xl
    even = jnp.concatenate([part_a[0, z_at, ys, x], part_b[0, ys, z_at, x], part_c[0, x, z_at, ys]], axis=1)
    odd = jnp.concatenate([part_a[1, ys, z_at, x], part_b[1, z_at, ys, x], part_c[1, x, ys, z_at]], axis=1)
    both = jnp.stack([even, odd], axis=1)
    return both.reshape(both.shape[0] * 2 * FEAT, TOK)


def combine(ref):
    most = jnp.max(ref[:, 0:2, :], axis=0)
    total = jnp.sum(ref[:, 2:4, :] * jnp.exp(ref[:, 0:2, :] - most), axis=0)
    return most, total, jnp.sum(ref[:, 4:6, :], axis=0)


def logits_kernel(
    part_a, part_b, part_c, table_ref, targets_ref,
    expo, stat, top_in, loss_ref,
    stat_in, part, part_in, more, more_in, top, send_sem, recv_sem,
):
    v, s = lax.axis_index("vocab"), lax.axis_index("seq")
    c, y, xh = lax.rem(v, 2), lax.rem(lax.div(v, 2), 8), lax.div(v, 16)
    z, xl_here = lax.rem(s, 8), lax.div(s, 8)
    side = (2 * xh + xl_here) * 2 + c

    def z_peer(r):
        return (v, xl_here * 8 + lax.rem(z + r, 8))

    def y_peer(r):
        return (xh * 16 + lax.rem(y + r, 8) * 2 + c, s)

    def x_peer(r):
        other = lax.rem(side + r, 8)
        x = lax.div(other, 2)
        return (lax.div(x, 2) * 16 + y * 2 + lax.rem(other, 2), lax.rem(x, 2) * 8 + z)

    barrier = pltpu.get_barrier_semaphore()

    def greet(r, carry):
        for peer in (z_peer(r), y_peer(r), x_peer(r)):
            pl.semaphore_signal(barrier, inc=1, device_id=peer, device_id_type=MESH)
        return carry

    lax.fori_loop(1, 8, greet, 0)

    def copy(phase, data, into, peer):
        pltpu.make_async_remote_copy(
            src_ref=data, dst_ref=into, send_sem=send_sem.at[phase], recv_sem=recv_sem.at[phase],
            device_id=peer, device_id_type=MESH,
        ).start()

    def logits_of(z_at):
        columns = []
        for xl in range(2):
            halves = [features_of((part_a, part_b, part_c), xh, xl, z_at, slice(None)) for xh in range(2)]
            columns.append(jnp.concatenate(halves, axis=0))
        return jnp.dot(table_ref[...], jnp.concatenate(columns, axis=1), preferred_element_type=F32)

    def statistics(z_at):
        values = expo[z_at]
        most = jnp.max(values, axis=0, keepdims=True)
        above = jnp.exp(values - most)
        total = jnp.sum(above, axis=0, keepdims=True)
        picked = jnp.sum(jnp.where(hit_of(targets_ref, z_at), values, 0.0), axis=0, keepdims=True)
        expo[z_at] = above
        for row, value in enumerate((most, total, picked)):
            for xl in range(2):
                stat[z_at, 2 * row + xl : 2 * row + xl + 1, :] = value[:, xl * TOK : (xl + 1) * TOK]

    first = lax.rem(side + 1, 8)
    expo[first] = logits_of(first)
    pl.semaphore_wait(barrier, 21)

    def step(i, carry):
        before, now = lax.rem(side + i, 8), lax.rem(side + 1 + i, 8)
        statistics(before)
        expo[now] = logits_of(now)
        copy(0, stat.at[before], stat_in.at[side], x_peer(i))
        return carry

    lax.fori_loop(1, 8, step, 0)
    statistics(side)
    stat_in[side] = stat[side]
    wait_bytes(stat_in.at[0:7], recv_sem.at[0])

    def merge(source, into):
        most, total, picked = combine(source)
        into[0:2, :] = most
        into[2:4, :] = total
        into[4:6, :] = picked

    merge(stat_in, part)
    for r in range(1, 8):
        copy(1, part, part_in.at[y], y_peer(r))
    part_in[y] = part[...]
    wait_bytes(part_in.at[0:7], recv_sem.at[1])
    merge(part_in, more)
    for r in range(1, 8):
        copy(2, more, more_in.at[z], z_peer(r))
    more_in[z] = more[...]
    wait_bytes(more_in.at[0:7], recv_sem.at[2])
    most, total, picked = combine(more_in)
    top[0:2, :] = most
    top[2:4, :] = 1.0 / total
    top[4:6, :] = most + jnp.log(total) - picked
    for r in range(1, 8):
        copy(3, top, top_in.at[side], x_peer(r))
    top_in[side] = top[...]
    wait_bytes(top_in.at[0:7], recv_sem.at[3])
    loss_ref[...] = jnp.where(xl_here == 0, top_in[z, 4:5, :], top_in[z, 5:6, :])
    for phase, data in enumerate((stat_in, part_in, more_in, top_in)):
        wait_bytes(data.at[0:7], send_sem.at[phase])


def head_kernel(
    part_a, part_b, part_c, expo, stat, top_in, targets_ref, emb_rows, emb_hot, loss_in,
    loss_ref, out_ref,
    score, out_v, out_sem,
):
    loss_ref[...] = loss_in[...]

    def score_step(z_at, carry):
        factor = jnp.exp(stat[z_at, 0:2, :] - top_in[z_at, 0:2, :]) * top_in[z_at, 2:4, :]
        factor = jnp.concatenate([factor[0:1, :], factor[1:2, :]], axis=1)
        value = expo[z_at] * factor - hit_of(targets_ref, z_at).astype(F32)
        score[0:ROWS, pl.ds(pl.multiple_of(z_at * 2 * TOK, 2 * TOK), 2 * TOK)] = value.astype(BF16)
        return carry

    lax.fori_loop(0, 8, score_step, 0)
    hot = emb_hot[...].astype(BF16)
    hot = jnp.concatenate([hot, hot, hot], axis=0)
    width = D // 4

    def head_step(i, carry):
        xh, ys = lax.div(i, 2), pl.ds(4 * lax.rem(i, 2), 4)
        columns = [features_of((part_a, part_b, part_c), xh, xl, z_at, ys) for z_at in range(8) for xl in range(2)]
        features = jnp.concatenate(columns, axis=1)
        at = pl.ds(pl.multiple_of(i * width, 128), width)
        turned = lax.dot_general(features, score[...], (((1,), (1,)), ((), ())), preferred_element_type=F32)
        total = jnp.transpose(turned)[0:ROWS, :]
        rest = emb_rows[:, at]
        high = rest.astype(BF16)
        rest = rest - high.astype(F32)
        middle = rest.astype(BF16)
        low = (rest - middle.astype(F32)).astype(BF16)
        terms = jnp.concatenate([high, middle, low], axis=0)
        total += lax.dot_general(hot, terms, (((0,), (0,)), ((), ())), preferred_element_type=F32)
        out_v[:, at] = total.astype(BF16)
        pltpu.make_async_copy(out_v.at[:, at], out_ref.at[:, at], out_sem).start()
        return carry

    lax.fori_loop(0, 4, head_step, 0)
    pltpu.make_async_copy(out_v, out_ref, out_sem).wait()


def on_device(hidden, table, targets, token_ids, input_grad):
    any_space = pl.BlockSpec(memory_space=pl.ANY)
    vmem = pl.BlockSpec(memory_space=pltpu.VMEM)
    dma = pltpu.SemaphoreType.DMA
    tile = pltpu.VMEM((8, TOK), F32)
    tiles = pltpu.VMEM((8, 8, TOK), F32)
    targets = targets.reshape(SEQ, TOK)
    *parts, emb_rows, emb_hot, table, targets = pl.pallas_call(
        gather_kernel,
        out_shape=(
            pltpu.VMEM((2, 8, 8, 4, LEN_A, TOK), BF16),
            pltpu.VMEM((2, 8, 8, 4, LEN_B, TOK), BF16),
            pltpu.VMEM((2, 4, 8, 8, LEN_C, TOK), BF16),
            pltpu.VMEM((SEQ, D), F32),
            pltpu.VMEM((SEQ, ROWS), F32),
            pltpu.VMEM((ROWS, D), BF16),
            pltpu.VMEM((SEQ, TOK), jnp.int32),
        ),
        in_specs=[any_space] * 5,
        out_specs=(vmem,) * 7,
        scratch_shapes=[
            pltpu.VMEM((1, TOK), jnp.int32),
            pltpu.VMEM((TOK, D), BF16),
            pltpu.VMEM((SEQ, 1, EXTRA), F32),
            pltpu.VMEM((SEQ, 1, EXTRA), F32),
            dma((len(ORDER),)),
            dma((len(PHASES),)),
            dma((2, 3)),
            dma((2,)),
            dma((7,)),
        ],
        compiler_params=pltpu.CompilerParams(collective_id=0, has_side_effects=True, vmem_limit_bytes=47 * 2**20),
        name="gather",
    )(hidden.T, token_ids.reshape(1, TOK), input_grad, table, targets)
    expo, stat, top_in, loss = pl.pallas_call(
        logits_kernel,
        out_shape=(pltpu.VMEM((8, ROWS, 2 * TOK), F32), tiles, tiles, pltpu.VMEM((1, TOK), F32)),
        in_specs=[vmem] * 5,
        out_specs=(vmem,) * 4,
        scratch_shapes=[tiles, tile, tiles, tile, tiles, tile, dma((4,)), dma((4,))],
        compiler_params=pltpu.CompilerParams(collective_id=1, has_side_effects=True, vmem_limit_bytes=24 * 2**20),
        cost_estimate=pl.CostEstimate(flops=2 * 2048 * ROWS * D, bytes_accessed=2**21, transcendentals=2048 * ROWS),
        name="logits",
    )(*parts, table, targets)
    loss, table_grad = pl.pallas_call(
        head_kernel,
        out_shape=(jax.ShapeDtypeStruct((1, TOK), F32), jax.ShapeDtypeStruct((ROWS, D), BF16)),
        in_specs=[vmem] * 10,
        out_specs=(vmem, any_space),
        scratch_shapes=[pltpu.VMEM((256, SEQ * TOK), BF16), pltpu.VMEM((ROWS, D), BF16), dma],
        compiler_params=pltpu.CompilerParams(vmem_limit_bytes=24 * 2**20),
        cost_estimate=pl.CostEstimate(flops=2 * 2048 * ROWS * D, bytes_accessed=2**21, transcendentals=2048 * ROWS),
        name="head",
    )(*parts, expo, stat, top_in, targets, emb_rows, emb_hot, loss)
    return loss.reshape(TOK), table_grad


def solution(mesh):
    in_specs = (P("seq", "vocab"), P(("vocab", "seq"), None), P(), P("seq"), P("seq", None))
    out_specs = (P("seq"), P(("vocab", "seq"), None))
    return jax.shard_map(
        on_device, mesh=mesh, in_specs=in_specs, out_specs=out_specs, check_vma=False
    )
```

time: 510 us -> 94.1 us (0.18)
  blocking collectives: 265 us -> 0 us
  waiting for transfers between devices: 184 us -> 0 us
  Pallas kernels: 0 us -> 93.3 us
  matrix products: 20.4 us -> 0 us
  other arithmetic: 17.4 us -> 0 us
  between operations: 14.8 us -> 0.65 us
  local copies, waits for them, and re-layouts: 7.57 us -> 0 us
    all_gather x2 -> x0, waiting for transfers between devices: 183 us -> none  [the longest x1 183 us: on_device(): piece = lax.all_gather(full_features, 'seq', axis=0, tiled=True)]
    pmax x1 -> x0, blocking collectives: 102 us -> none  [on_device(): top_all = lax.pmax(local_top, ('vocab', 'seq'))]
    psum x1 -> x0, blocking collectives: 94.7 us -> none  [on_device(): lax.psum((local_total, local_pick), ('vocab', 'seq'))]
    pallas_call x0 -> x3, Pallas kernels: none -> 93.3 us  [the longest x1 60.8 us: on_device(): pl.pallas_call(gather_kernel, out_shape=(pltpu.VMEM((2, 8, 8, 4, LEN_A, T...]
    all_gather x1 -> x0, blocking collectives: 49.8 us -> none  [on_device(): full_features = lax.all_gather(hidden, 'vocab', axis=1, tiled=True)]
    dot_general x2 -> x0, matrix products: 20.4 us -> none  [the longest x1 11.7 us: on_device(): lax.dot_general(score_grad, hidden_all, (((0,), (0,)), ((), ())), preferr...]
    unnamed x1 -> x0, blocking collectives: 18.4 us -> none
    scatter-add x1 -> x0, other arithmetic: 9.14 us -> none  [on_device(): embed_grad = jnp.zeros((rows_here, width), jnp.float32).at[target_rows].a...]
  transfers between devices with their start and end apart: 2 -> 0, of which waited for: 2 -> 0; matrix products, arithmetic and copies ran while one was open for 1% -> 0% of each run, Pallas kernels for 0% -> 0%
where the time goes in v2:
time: 94.1 us; the launch traced here: 93.9 us
  Pallas kernels  93.3 us (99%)
    pallas_call x1, Pallas kernels, on_device(): pl.pallas_call(gather_kernel, out_shape=(pltpu.VMEM((2, 8, 8, 4, LEN_A, T...  60.8 us
    pallas_call x1, Pallas kernels, on_device(): pl.pallas_call(logits_kernel, out_shape=(pltpu.VMEM((8, ROWS, 2 * TOK), F...  25.4 us
    pallas_call x1, Pallas kernels, on_device(): pl.pallas_call(head_kernel, out_shape=(jax.ShapeDtypeStruct((1, TOK), F32...  7.07 us

profile of v2, /device:TPU:1, one launch (start us, length us, event | category | flops | bytes accessed | tf_op | source)
XLA Modules:
  0.0 93.9 jit_solution(11189994347214628664)
XLA Ops:
  0.6 60.8 %gather.1 = (bf16[2,8,8,4,32,128]{5,4,3,2,1,0:T(8,128)(2,1)S(1)}, bf16[2,8,8,4,32,128]{5,4,3,2,1,0:T(8,128)(2,1)S(1)}, bf16[2,4,8,8,48,128]{5,4,3,2,1,0:T(8,128)...) custom-call(bf16[112,128]{1,0:T(8,128)(2,1)} %bitcast.4, ...), custom_call_target="tpu_custom_call" | custom-call | tf_op jit(solution)/shard_map/gather/pallas_call | solution.py:465
  61.5 25.4 %logits.1 = (f32[8,250,256]{2,1,0:T(8,128)S(1)}, f32[8,8,128]{2,1,0:T(8,128)S(1)}, f32[8,8,128]{2,1,0:T(8,128)S(1)}, f32[1,128]{1,0:T(1,128)S(1)}) custom-call(bf16[2,8,8,4,32,128]{5,4,3,2,1,0:T(8,128)(2,1)S(1)} %get-tuple-element.15.part_a, bf16[2,8,8,4,32,128]{5,4,3,2,1,0:T(8,128)(2,1)S(1)} %get-tuple-element.16.part_b, ...), custom_call_target="tpu_custom_call" | custom-call | flops 3670016000 | bytes 2097152 | tf_op jit(solution)/shard_map/logits/pallas_call | solution.py:492
  86.8 7.1 %head.1 = (f32[1,128]{1,0:T(1,128)}, bf16[250,3584]{1,0:T(8,128)(2,1)}) custom-call(bf16[2,8,8,4,32,128]{5,4,3,2,1,0:T(8,128)(2,1)S(1)} %get-tuple-element.15.part_a, bf16[2,8,8,4,32,128]{5,4,3,2,1,0:T(8,128)(2,1)S(1)} %get-tuple-element.16.part_b, bf16[2,4,8,8,48,128]{5,4,3,2,1,0:T(8,128)(2,1)S(1)} %get-tuple-element.17.part_c, ...), custom_call_target="tpu_custom_call" | custom-call | flops 3670016000 | bytes 2097152 | tf_op jit(solution)/shard_map/head/pallas_call | solution.py:502

commit v3 on v2

--- a/solution.py
+++ b/solution.py
@@ -258,7 +258,7 @@
 
     def embed_arrived():
         wait_bytes(emb_in.at[pl.ds(0, SEQ - 1)], emb_sem.at[1])
-        lane_ids = lax.broadcasted_iota(jnp.int32, (1, ROWS), 1).astype(F32)
+        lane_ids = lax.broadcasted_iota(jnp.int32, (1, 256), 1).astype(F32)
         for j in range(SEQ):
             emb_rows[j : j + 1, :] = emb_in[j, :, 0:D]
             emb_hot[j : j + 1, :] = (lane_ids == emb_in[j, :, D : D + 1]).astype(F32)
@@ -293,11 +293,10 @@
             wait_bytes(data.at[1 - c] if side else data.at[c], core_sem.at[side, i])
 
 
-def hit_of(targets_ref, z_at):
+def hit_of(targets_ref, xl, z_at):
     row_start = (lax.axis_index("vocab") * SEQ + lax.axis_index("seq")) * ROWS
-    row_ids = lax.broadcasted_iota(jnp.int32, (ROWS, 2 * TOK), 0)
-    both = jnp.concatenate([targets_ref[pl.ds(8 * xl + z_at, 1), :] for xl in range(2)], axis=1)
-    return (both - row_start) == row_ids
+    row_ids = lax.broadcasted_iota(jnp.int32, (ROWS, TOK), 0)
+    return (targets_ref[pl.ds(8 * xl + z_at, 1), :] - row_start) == row_ids
 
 
 def features_of(parts, xh, xl, z_at, ys):
@@ -310,16 +309,33 @@
 
 
 def combine(ref):
-    most = jnp.max(ref[:, 0:2, :], axis=0)
-    total = jnp.sum(ref[:, 2:4, :] * jnp.exp(ref[:, 0:2, :] - most), axis=0)
-    return most, total, jnp.sum(ref[:, 4:6, :], axis=0)
+    most = jnp.max(ref[:, 0:1, :], axis=0)
+    total = jnp.sum(ref[:, 1:2, :] * jnp.exp(ref[:, 0:1, :] - most), axis=0)
+    return most, total, jnp.sum(ref[:, 2:3, :], axis=0)
+
+
+def fill_score(xl, expo, stat, top_in, targets_ref, score):
+    def step(z_at, carry):
+        factor = jnp.exp(stat[xl, z_at, 0:1, :] - top_in[xl, z_at, 0:1, :]) * top_in[xl, z_at, 1:2, :]
+        value = expo[xl, z_at] * factor - hit_of(targets_ref, xl, z_at).astype(F32)
+        score[0:ROWS, pl.ds(pl.multiple_of(z_at * TOK, TOK), TOK)] = value.astype(BF16)
+        return carry
+
+    lax.fori_loop(0, 8, step, 0)
+
+
+def head_block(parts, xl, i, score):
+    xh, ys = lax.div(i, 2), pl.ds(4 * lax.rem(i, 2), 4)
+    features = jnp.concatenate([features_of(parts, xh, xl, z_at, ys) for z_at in range(8)], axis=1)
+    return lax.dot_general(features, score[...], (((1,), (1,)), ((), ())), preferred_element_type=F32)
 
 
 def logits_kernel(
-    part_a, part_b, part_c, table_ref, targets_ref,
-    expo, stat, top_in, loss_ref,
-    stat_in, part, part_in, more, more_in, top, send_sem, recv_sem,
+    part_a, part_b, part_c, table_ref, targets_ref, emb_rows, emb_hot,
+    expo, stat, top_in, loss_ref, turned,
+    stat_in, part, part_in, more, more_in, top, score, send_sem, recv_sem,
 ):
+    parts = (part_a, part_b, part_c)
     v, s = lax.axis_index("vocab"), lax.axis_index("seq")
     c, y, xh = lax.rem(v, 2), lax.rem(lax.div(v, 2), 8), lax.div(v, 16)
     z, xl_here = lax.rem(s, 8), lax.div(s, 8)
@@ -345,109 +361,126 @@
 
     lax.fori_loop(1, 8, greet, 0)
 
-    def copy(phase, data, into, peer):
+    def copy(xl, phase, data, into, peer):
         pltpu.make_async_remote_copy(
-            src_ref=data, dst_ref=into, send_sem=send_sem.at[phase], recv_sem=recv_sem.at[phase],
+            src_ref=data, dst_ref=into, send_sem=send_sem.at[xl, phase], recv_sem=recv_sem.at[xl, phase],
             device_id=peer, device_id_type=MESH,
         ).start()
 
-    def logits_of(z_at):
-        columns = []
-        for xl in range(2):
-            halves = [features_of((part_a, part_b, part_c), xh, xl, z_at, slice(None)) for xh in range(2)]
-            columns.append(jnp.concatenate(halves, axis=0))
-        return jnp.dot(table_ref[...], jnp.concatenate(columns, axis=1), preferred_element_type=F32)
-
-    def statistics(z_at):
-        values = expo[z_at]
-        most = jnp.max(values, axis=0, keepdims=True)
-        above = jnp.exp(values - most)
-        total = jnp.sum(above, axis=0, keepdims=True)
-        picked = jnp.sum(jnp.where(hit_of(targets_ref, z_at), values, 0.0), axis=0, keepdims=True)
-        expo[z_at] = above
-        for row, value in enumerate((most, total, picked)):
-            for xl in range(2):
-                stat[z_at, 2 * row + xl : 2 * row + xl + 1, :] = value[:, xl * TOK : (xl + 1) * TOK]
-
-    first = lax.rem(side + 1, 8)
-    expo[first] = logits_of(first)
+    def blocks_of(n):
+        xl, m = lax.div(n, 4), lax.rem(n, 4)
+        return xl, m, [lax.rem(side + 1 + 2 * m + k, 8) for k in range(2)]
+
+    def logits_step(n):
+        xl, _, blocks = blocks_of(n)
+        columns = [
+            jnp.concatenate([features_of(parts, half, xl, z_at, slice(None)) for half in range(2)], axis=0)
+            for z_at in blocks
+        ]
+        values = jnp.dot(table_ref[...], jnp.concatenate(columns, axis=1), preferred_element_type=F32)
+        for k, z_at in enumerate(blocks):
+            expo[xl, z_at] = values[:, k * TOK : (k + 1) * TOK]
+
+    def statistics_step(n):
+        xl, _, blocks = blocks_of(n)
+        for z_at in blocks:
+            values = expo[xl, z_at]
+            most = jnp.max(values, axis=0, keepdims=True)
+            above = jnp.exp(values - most)
+            stat[xl, z_at, 0:1, :] = most
+            stat[xl, z_at, 1:2, :] = jnp.sum(above, axis=0, keepdims=True)
+            hit = hit_of(targets_ref, xl, z_at)
+            stat[xl, z_at, 2:3, :] = jnp.sum(jnp.where(hit, values, 0.0), axis=0, keepdims=True)
+            expo[xl, z_at] = above
+
+    def send_step(n):
+        xl, m, blocks = blocks_of(n)
+        copy(xl, 0, stat.at[xl, blocks[0]], stat_in.at[xl, side], x_peer(1 + 2 * m))
+
+        @pl.when(m < 3)
+        def _():
+            copy(xl, 0, stat.at[xl, blocks[1]], stat_in.at[xl, side], x_peer(2 + 2 * m))
+
+    logits_step(jnp.int32(0))
     pl.semaphore_wait(barrier, 21)
 
-    def step(i, carry):
-        before, now = lax.rem(side + i, 8), lax.rem(side + 1 + i, 8)
-        statistics(before)
-        expo[now] = logits_of(now)
-        copy(0, stat.at[before], stat_in.at[side], x_peer(i))
+    def step(n, carry):
+        statistics_step(n - 1)
+        logits_step(n)
+        send_step(n - 1)
         return carry
 
     lax.fori_loop(1, 8, step, 0)
-    statistics(side)
-    stat_in[side] = stat[side]
-    wait_bytes(stat_in.at[0:7], recv_sem.at[0])
+    statistics_step(jnp.int32(7))
+    send_step(jnp.int32(7))
 
     def merge(source, into):
         most, total, picked = combine(source)
-        into[0:2, :] = most
-        into[2:4, :] = total
-        into[4:6, :] = picked
-
-    merge(stat_in, part)
-    for r in range(1, 8):
-        copy(1, part, part_in.at[y], y_peer(r))
-    part_in[y] = part[...]
-    wait_bytes(part_in.at[0:7], recv_sem.at[1])
-    merge(part_in, more)
-    for r in range(1, 8):
-        copy(2, more, more_in.at[z], z_peer(r))
-    more_in[z] = more[...]
-    wait_bytes(more_in.at[0:7], recv_sem.at[2])
-    most, total, picked = combine(more_in)
-    top[0:2, :] = most
-    top[2:4, :] = 1.0 / total
-    top[4:6, :] = most + jnp.log(total) - picked
-    for r in range(1, 8):
-        copy(3, top, top_in.at[side], x_peer(r))
-    top_in[side] = top[...]
-    wait_bytes(top_in.at[0:7], recv_sem.at[3])
-    loss_ref[...] = jnp.where(xl_here == 0, top_in[z, 4:5, :], top_in[z, 5:6, :])
-    for phase, data in enumerate((stat_in, part_in, more_in, top_in)):
-        wait_bytes(data.at[0:7], send_sem.at[phase])
-
-
-def head_kernel(
-    part_a, part_b, part_c, expo, stat, top_in, targets_ref, emb_rows, emb_hot, loss_in,
-    loss_ref, out_ref,
-    score, out_v, out_sem,
-):
-    loss_ref[...] = loss_in[...]
-
-    def score_step(z_at, carry):
-        factor = jnp.exp(stat[z_at, 0:2, :] - top_in[z_at, 0:2, :]) * top_in[z_at, 2:4, :]
-        factor = jnp.concatenate([factor[0:1, :], factor[1:2, :]], axis=1)
-        value = expo[z_at] * factor - hit_of(targets_ref, z_at).astype(F32)
-        score[0:ROWS, pl.ds(pl.multiple_of(z_at * 2 * TOK, 2 * TOK), 2 * TOK)] = value.astype(BF16)
-        return carry
-
-    lax.fori_loop(0, 8, score_step, 0)
+        into[0:1, :] = most
+        into[1:2, :] = total
+        into[2:3, :] = picked
+
+    for xl in range(2):
+        stat_in[xl, side] = stat[xl, side]
+        wait_bytes(stat_in.at[xl, 0:7], recv_sem.at[xl, 0])
+        merge(stat_in.at[xl], part.at[xl])
+        for r in range(1, 8):
+            copy(xl, 1, part.at[xl], part_in.at[xl, y], y_peer(r))
+        part_in[xl, y] = part[xl]
+    for xl in range(2):
+        wait_bytes(part_in.at[xl, 0:7], recv_sem.at[xl, 1])
+        merge(part_in.at[xl], more.at[xl])
+        for r in range(1, 8):
+            copy(xl, 2, more.at[xl], more_in.at[xl, z], z_peer(r))
+        more_in[xl, z] = more[xl]
+    for xl in range(2):
+        wait_bytes(more_in.at[xl, 0:7], recv_sem.at[xl, 2])
+        most, total, picked = combine(more_in.at[xl])
+        top[xl, 0:1, :] = most
+        top[xl, 1:2, :] = 1.0 / total
+        top[xl, 2:3, :] = most + jnp.log(total) - picked
+        for r in range(1, 8):
+            copy(xl, 3, top.at[xl], top_in.at[xl, side], x_peer(r))
+        top_in[xl, side] = top[xl]
+
     hot = emb_hot[...].astype(BF16)
     hot = jnp.concatenate([hot, hot, hot], axis=0)
-    width = D // 4
+    wait_bytes(top_in.at[0, 0:7], recv_sem.at[0, 3])
+    fill_score(0, expo, stat, top_in, targets_ref, score)
 
     def head_step(i, carry):
-        xh, ys = lax.div(i, 2), pl.ds(4 * lax.rem(i, 2), 4)
-        columns = [features_of((part_a, part_b, part_c), xh, xl, z_at, ys) for z_at in range(8) for xl in range(2)]
-        features = jnp.concatenate(columns, axis=1)
-        at = pl.ds(pl.multiple_of(i * width, 128), width)
-        turned = lax.dot_general(features, score[...], (((1,), (1,)), ((), ())), preferred_element_type=F32)
-        total = jnp.transpose(turned)[0:ROWS, :]
+        at = pl.ds(pl.multiple_of(i * (D // 4), 128), D // 4)
         rest = emb_rows[:, at]
         high = rest.astype(BF16)
         rest = rest - high.astype(F32)
         middle = rest.astype(BF16)
         low = (rest - middle.astype(F32)).astype(BF16)
         terms = jnp.concatenate([high, middle, low], axis=0)
-        total += lax.dot_general(hot, terms, (((0,), (0,)), ((), ())), preferred_element_type=F32)
-        out_v[:, at] = total.astype(BF16)
+        embed = lax.dot_general(terms, hot, (((0,), (0,)), ((), ())), preferred_element_type=F32)
+        turned[i] = head_block(parts, 0, i, score) + embed
+        return carry
+
+    lax.fori_loop(0, 4, head_step, 0)
+    wait_bytes(top_in.at[1, 0:7], recv_sem.at[1, 3])
+    loss_ref[...] = top_in[xl_here, z, 2:3, :]
+    for xl in range(2):
+        for phase, data in enumerate((stat_in, part_in, more_in, top_in)):
+            wait_bytes(data.at[xl, 0:7], send_sem.at[xl, phase])
+
+
+def head_kernel(
+    part_a, part_b, part_c, expo, stat, top_in, targets_ref, turned, loss_in,
+    loss_ref, out_ref,
+    score, out_v, out_sem,
+):
+    parts = (part_a, part_b, part_c)
+    loss_ref[...] = loss_in[...]
+    fill_score(1, expo, stat, top_in, targets_ref, score)
+
+    def head_step(i, carry):
+        at = pl.ds(pl.multiple_of(i * (D // 4), 128), D // 4)
+        total = jnp.transpose(turned[i] + head_block(parts, 1, i, score))
+        out_v[:, at] = total[0:ROWS, :].astype(BF16)
         pltpu.make_async_copy(out_v.at[:, at], out_ref.at[:, at], out_sem).start()
         return carry
 
@@ -459,8 +492,8 @@
     any_space = pl.BlockSpec(memory_space=pl.ANY)
     vmem = pl.BlockSpec(memory_space=pltpu.VMEM)
     dma = pltpu.SemaphoreType.DMA
-    tile = pltpu.VMEM((8, TOK), F32)
-    tiles = pltpu.VMEM((8, 8, TOK), F32)
+    tile = pltpu.VMEM((2, 8, TOK), F32)
+    tiles = pltpu.VMEM((2, 8, 8, TOK), F32)
     targets = targets.reshape(SEQ, TOK)
     *parts, emb_rows, emb_hot, table, targets = pl.pallas_call(
         gather_kernel,
@@ -469,7 +502,7 @@
             pltpu.VMEM((2, 8, 8, 4, LEN_B, TOK), BF16),
             pltpu.VMEM((2, 4, 8, 8, LEN_C, TOK), BF16),
             pltpu.VMEM((SEQ, D), F32),
-            pltpu.VMEM((SEQ, ROWS), F32),
+            pltpu.VMEM((SEQ, 256), F32),
             pltpu.VMEM((ROWS, D), BF16),
             pltpu.VMEM((SEQ, TOK), jnp.int32),
         ),
@@ -489,26 +522,30 @@
         compiler_params=pltpu.CompilerParams(collective_id=0, has_side_effects=True, vmem_limit_bytes=47 * 2**20),
         name="gather",
     )(hidden.T, token_ids.reshape(1, TOK), input_grad, table, targets)
-    expo, stat, top_in, loss = pl.pallas_call(
+    expo, stat, top_in, loss, turned = pl.pallas_call(
         logits_kernel,
-        out_shape=(pltpu.VMEM((8, ROWS, 2 * TOK), F32), tiles, tiles, pltpu.VMEM((1, TOK), F32)),
-        in_specs=[vmem] * 5,
-        out_specs=(vmem,) * 4,
-        scratch_shapes=[tiles, tile, tiles, tile, tiles, tile, dma((4,)), dma((4,))],
+        out_shape=(
+            pltpu.VMEM((2, 8, ROWS, TOK), F32), tiles, tiles, pltpu.VMEM((1, TOK), F32), pltpu.VMEM((4, D // 4, 256), F32),
+        ),
+        in_specs=[vmem] * 7,
+        out_specs=(vmem,) * 5,
+        scratch_shapes=[
+            tiles, tile, tiles, tile, tiles, tile, pltpu.VMEM((256, 8 * TOK), BF16), dma((2, 4)), dma((2, 4)),
+        ],
         compiler_params=pltpu.CompilerParams(collective_id=1, has_side_effects=True, vmem_limit_bytes=24 * 2**20),
         cost_estimate=pl.CostEstimate(flops=2 * 2048 * ROWS * D, bytes_accessed=2**21, transcendentals=2048 * ROWS),
         name="logits",
-    )(*parts, table, targets)
+    )(*parts, table, targets, emb_rows, emb_hot)
     loss, table_grad = pl.pallas_call(
         head_kernel,
         out_shape=(jax.ShapeDtypeStruct((1, TOK), F32), jax.ShapeDtypeStruct((ROWS, D), BF16)),
-        in_specs=[vmem] * 10,
+        in_specs=[vmem] * 9,
         out_specs=(vmem, any_space),
-        scratch_shapes=[pltpu.VMEM((256, SEQ * TOK), BF16), pltpu.VMEM((ROWS, D), BF16), dma],
+        scratch_shapes=[pltpu.VMEM((256, 8 * TOK), BF16), pltpu.VMEM((ROWS, D), BF16), dma],
         compiler_params=pltpu.CompilerParams(vmem_limit_bytes=24 * 2**20),
         cost_estimate=pl.CostEstimate(flops=2 * 2048 * ROWS * D, bytes_accessed=2**21, transcendentals=2048 * ROWS),
         name="head",
-    )(*parts, expo, stat, top_in, targets, emb_rows, emb_hot, loss)
+    )(*parts, expo, stat, top_in, targets, turned, loss)
     return loss.reshape(TOK), table_grad
 
 

time: 94.1 us -> 93.1 us (0.989)
  Pallas kernels: 93.3 us -> 92.3 us
    pallas_call x1, Pallas kernels: 7.07 us -> 4.6 us  [on_device(): pl.pallas_call(head_kernel, out_shape=(jax.ShapeDtypeStruct((1, TOK), F32...]
    pallas_call x1, Pallas kernels: 25.4 us -> 26.8 us  [on_device(): pl.pallas_call(logits_kernel, out_shape=(pltpu.VMEM((2, 8, ROWS, TOK), F3...]
where the time goes in v3:
time: 93.1 us; the launch traced here: 92.9 us
  Pallas kernels  92.3 us (99%)
    pallas_call x1, Pallas kernels, on_device(): pl.pallas_call(gather_kernel, out_shape=(pltpu.VMEM((2, 8, 8, 4, LEN_A, T...  60.8 us
    pallas_call x1, Pallas kernels, on_device(): pl.pallas_call(logits_kernel, out_shape=(pltpu.VMEM((2, 8, ROWS, TOK), F3...  26.8 us
    pallas_call x1, Pallas kernels, on_device(): pl.pallas_call(head_kernel, out_shape=(jax.ShapeDtypeStruct((1, TOK), F32...  4.6 us

profile of v3, /device:TPU:1, one launch (start us, length us, event | category | flops | bytes accessed | tf_op | source)
XLA Modules:
  0.0 92.9 jit_solution(13216385878947218424)
XLA Ops:
  0.6 60.8 %gather.1 = (bf16[2,8,8,4,32,128]{5,4,3,2,1,0:T(8,128)(2,1)S(1)}, bf16[2,8,8,4,32,128]{5,4,3,2,1,0:T(8,128)(2,1)S(1)}, bf16[2,4,8,8,48,128]{5,4,3,2,1,0:T(8,128)...) custom-call(bf16[112,128]{1,0:T(8,128)(2,1)} %bitcast.4, ...), custom_call_target="tpu_custom_call" | custom-call | tf_op jit(solution)/shard_map/gather/pallas_call | solution.py:498
  61.5 26.8 %logits.1 = (f32[2,8,250,128]{3,2,1,0:T(8,128)S(1)}, f32[2,8,8,128]{3,2,1,0:T(8,128)S(1)}, f32[2,8,8,128]{3,2,1,0:T(8,128)S(1)}, f32[1,128]{1,0:T(1,128)S(1)}, f32[4,896,256]{2,1,0:T(8,128)S(1)}) custom-call(bf16[2,8,8,4,32,128]{5,4,3,2,1,0:T(8,128)(2,1)S(1)} %get-tuple-element.16.part_a, bf16[2,8,8,4,32,128]{5,4,3,2,1,0:T(8,128)(2,1)S(1)} %get-tuple-element.17.part_b, ...), custom_call_target="tpu_custom_call" | custom-call | flops 3670016000 | bytes 2097152 | tf_op jit(solution)/shard_map/logits/pallas_call | solution.py:525
  88.3 4.6 %head.1 = (f32[1,128]{1,0:T(1,128)}, bf16[250,3584]{1,0:T(8,128)(2,1)}) custom-call(bf16[2,8,8,4,32,128]{5,4,3,2,1,0:T(8,128)(2,1)S(1)} %get-tuple-element.16.part_a, bf16[2,8,8,4,32,128]{5,4,3,2,1,0:T(8,128)(2,1)S(1)} %get-tuple-element.17.part_b, bf16[2,4,8,8,48,128]{5,4,3,2,1,0:T(8,128)(2,1)S(1)} %get-tuple-element.18.part_c, ...), custom_call_target="tpu_custom_call" | custom-call | flops 3670016000 | bytes 2097152 | tf_op jit(solution)/shard_map/head/pallas_call | solution.py:539

commit v4 on v3

--- a/solution.py
+++ b/solution.py
@@ -1,3 +1,4 @@
+import functools
 import heapq
 import itertools
 
@@ -124,12 +125,14 @@
     pltpu.make_async_copy(data, data, sem).wait()
 
 
-def gather_kernel(
-    hidden_ref, ids_hbm, input_grad_ref, table_ref, targets_ref,
-    part_a, part_b, part_c, emb_rows, emb_hot, table_v, targets_v,
-    ids_ref, grad_v, emb_out, emb_in,
-    recv_sem, send_sem, core_sem, emb_sem, local_sem,
+def main_kernel(
+    hidden_ref, ids_hbm, input_grad_ref, table_ref, targets_hbm,
+    part_a, part_b, part_c, targets_ref, expo, stat, top_in, loss_ref, turned,
+    table_v, table_c, ids_ref, grad_v, emb_out, emb_in, emb_rows, emb_hot,
+    stat_in, part, part_in, more, more_in, top, score,
+    recv_sem, send_sem, core_sem, emb_sem, local_sem, round_send, round_recv,
 ):
+    parts = (part_a, part_b, part_c)
     v, s = lax.axis_index("vocab"), lax.axis_index("seq")
     c = lax.rem(v, 2)
     y = lax.rem(lax.div(v, 2), 8)
@@ -156,7 +159,7 @@
     ]
     ids_copy = pltpu.make_async_copy(ids_hbm, ids_ref, local_sem.at[3])
     grad_copy = pltpu.make_async_copy(input_grad_ref, grad_v, local_sem.at[4])
-    targets_copy = pltpu.make_async_copy(targets_ref, targets_v, local_sem.at[5])
+    targets_copy = pltpu.make_async_copy(targets_hbm, targets_ref, local_sem.at[5])
     table_copy = pltpu.make_async_copy(table_ref, table_v, local_sem.at[6])
     for copy in own:
         copy.start()
@@ -263,6 +266,18 @@
             emb_rows[j : j + 1, :] = emb_in[j, :, 0:D]
             emb_hot[j : j + 1, :] = (lane_ids == emb_in[j, :, D : D + 1]).astype(F32)
 
+    def split_columns(core, j):
+        n0 = 256 * j
+        low = (n0 + FEAT * (n0 // FEAT) + FEAT * core) // 128 * 128
+        width = min(768, D - low)
+        n = lax.broadcasted_iota(jnp.int32, (width, 256), 1) + n0
+        chunk = sum((n >= FEAT * k).astype(jnp.int32) for k in range(n0 // FEAT + 1, (n0 + 255) // FEAT + 1))
+        source = n + FEAT * (chunk + n0 // FEAT + core) - low
+        pick = (lax.broadcasted_iota(jnp.int32, (width, 256), 0) == source).astype(F32).astype(BF16)
+        columns = jnp.dot(table_v[:, low : low + width], pick, preferred_element_type=F32)
+        table_c[core, :, n0 : n0 + 256] = columns.astype(BF16)
+
+    splits = [(core, j) for core in range(2) for j in range(HALF // 256)]
     send_ready()
     embedded = False
     needed = {key for key in MESSAGES if key[0] in ("XA", "XB", "AQ", "BP")}
@@ -273,73 +288,16 @@
         if not embedded and needed <= done:
             embedded = True
             embed_rows()
+        if len(done) == 20:
+            table_copy.wait()
+        if len(done) > 20 and splits:
+            split_columns(*splits.pop(0))
         if len(done) == len(ORDER) * 4 // 5:
             embed_arrived()
 
     targets_copy.wait()
-    table_copy.wait()
-    wait_bytes(a.at[p, q, 0:3], send_sem.at[0])
-    wait_bytes(b.at[q, p, 0:3], send_sem.at[1])
-    wait_bytes(cc.at[x, p, 0:7], send_sem.at[2])
-    wait_bytes(cc.at[x, 0:7], send_sem.at[3])
-    wait_bytes(cc.at[0:3], send_sem.at[4])
-    wait_bytes(a.at[p, 0:7], send_sem.at[5])
-    wait_bytes(b.at[q, 0:7], send_sem.at[6])
-    wait_bytes(a.at[0:7], send_sem.at[7])
-    wait_bytes(b.at[0:7], send_sem.at[8])
-    wait_bytes(emb_out.at[pl.ds(0, SEQ - 1)], emb_sem.at[0])
-    for side in (0, 1):
-        for i, data in enumerate((part_a, part_b, part_c)):
-            wait_bytes(data.at[1 - c] if side else data.at[c], core_sem.at[side, i])
-
-
-def hit_of(targets_ref, xl, z_at):
-    row_start = (lax.axis_index("vocab") * SEQ + lax.axis_index("seq")) * ROWS
-    row_ids = lax.broadcasted_iota(jnp.int32, (ROWS, TOK), 0)
-    return (targets_ref[pl.ds(8 * xl + z_at, 1), :] - row_start) == row_ids
-
-
-def features_of(parts, xh, xl, z_at, ys):
-    part_a, part_b, part_c = parts
-    x = 2 * xh + xl
-    even = jnp.concatenate([part_a[0, z_at, ys, x], part_b[0, ys, z_at, x], part_c[0, x, z_at, ys]], axis=1)
-    odd = jnp.concatenate([part_a[1, ys, z_at, x], part_b[1, z_at, ys, x], part_c[1, x, ys, z_at]], axis=1)
-    both = jnp.stack([even, odd], axis=1)
-    return both.reshape(both.shape[0] * 2 * FEAT, TOK)
-
-
-def combine(ref):
-    most = jnp.max(ref[:, 0:1, :], axis=0)
-    total = jnp.sum(ref[:, 1:2, :] * jnp.exp(ref[:, 0:1, :] - most), axis=0)
-    return most, total, jnp.sum(ref[:, 2:3, :], axis=0)
-
-
-def fill_score(xl, expo, stat, top_in, targets_ref, score):
-    def step(z_at, carry):
-        factor = jnp.exp(stat[xl, z_at, 0:1, :] - top_in[xl, z_at, 0:1, :]) * top_in[xl, z_at, 1:2, :]
-        value = expo[xl, z_at] * factor - hit_of(targets_ref, xl, z_at).astype(F32)
-        score[0:ROWS, pl.ds(pl.multiple_of(z_at * TOK, TOK), TOK)] = value.astype(BF16)
-        return carry
-
-    lax.fori_loop(0, 8, step, 0)
-
-
-def head_block(parts, xl, i, score):
-    xh, ys = lax.div(i, 2), pl.ds(4 * lax.rem(i, 2), 4)
-    features = jnp.concatenate([features_of(parts, xh, xl, z_at, ys) for z_at in range(8)], axis=1)
-    return lax.dot_general(features, score[...], (((1,), (1,)), ((), ())), preferred_element_type=F32)
-
-
-def logits_kernel(
-    part_a, part_b, part_c, table_ref, targets_ref, emb_rows, emb_hot,
-    expo, stat, top_in, loss_ref, turned,
-    stat_in, part, part_in, more, more_in, top, score, send_sem, recv_sem,
-):
-    parts = (part_a, part_b, part_c)
-    v, s = lax.axis_index("vocab"), lax.axis_index("seq")
-    c, y, xh = lax.rem(v, 2), lax.rem(lax.div(v, 2), 8), lax.div(v, 16)
-    z, xl_here = lax.rem(s, 8), lax.div(s, 8)
-    side = (2 * xh + xl_here) * 2 + c
+    xh, xl_here = lax.div(x, 2), lax.rem(x, 2)
+    side = 2 * x + c
 
     def z_peer(r):
         return (v, xl_here * 8 + lax.rem(z + r, 8))
@@ -352,18 +310,9 @@
         x = lax.div(other, 2)
         return (lax.div(x, 2) * 16 + y * 2 + lax.rem(other, 2), lax.rem(x, 2) * 8 + z)
 
-    barrier = pltpu.get_barrier_semaphore()
-
-    def greet(r, carry):
-        for peer in (z_peer(r), y_peer(r), x_peer(r)):
-            pl.semaphore_signal(barrier, inc=1, device_id=peer, device_id_type=MESH)
-        return carry
-
-    lax.fori_loop(1, 8, greet, 0)
-
     def copy(xl, phase, data, into, peer):
         pltpu.make_async_remote_copy(
-            src_ref=data, dst_ref=into, send_sem=send_sem.at[xl, phase], recv_sem=recv_sem.at[xl, phase],
+            src_ref=data, dst_ref=into, send_sem=round_send.at[xl, phase], recv_sem=round_recv.at[xl, phase],
             device_id=peer, device_id_type=MESH,
         ).start()
 
@@ -371,15 +320,14 @@
         xl, m = lax.div(n, 4), lax.rem(n, 4)
         return xl, m, [lax.rem(side + 1 + 2 * m + k, 8) for k in range(2)]
 
-    def logits_step(n):
+    def logits_step(n, core):
         xl, _, blocks = blocks_of(n)
         columns = [
-            jnp.concatenate([features_of(parts, half, xl, z_at, slice(None)) for half in range(2)], axis=0)
+            jnp.concatenate([core_features(parts, core, half, xl, z_at, slice(None)).reshape(HALF // 2, TOK) for half in range(2)], axis=0)
             for z_at in blocks
         ]
-        values = jnp.dot(table_ref[...], jnp.concatenate(columns, axis=1), preferred_element_type=F32)
-        for k, z_at in enumerate(blocks):
-            expo[xl, z_at] = values[:, k * TOK : (k + 1) * TOK]
+        values = jnp.dot(table_c[core], jnp.concatenate(columns, axis=1), preferred_element_type=F32)
+        return xl, [(z_at, values[:, k * TOK : (k + 1) * TOK]) for k, z_at in enumerate(blocks)]
 
     def statistics_step(n):
         xl, _, blocks = blocks_of(n)
@@ -401,16 +349,36 @@
         def _():
             copy(xl, 0, stat.at[xl, blocks[1]], stat_in.at[xl, side], x_peer(2 + 2 * m))
 
-    logits_step(jnp.int32(0))
-    pl.semaphore_wait(barrier, 21)
-
-    def step(n, carry):
-        statistics_step(n - 1)
-        logits_step(n)
-        send_step(n - 1)
-        return carry
-
-    lax.fori_loop(1, 8, step, 0)
+    def first_pass(core):
+        def step(n, carry):
+            xl, values = logits_step(n, core)
+            for z_at, value in values:
+                expo[xl, z_at] = value
+            return carry
+
+        lax.fori_loop(0, 8, step, 0)
+
+    def second_pass(core):
+        def add(n):
+            xl, values = logits_step(n, core)
+            for z_at, value in values:
+                expo[xl, z_at] += value
+
+        def step(n, carry):
+            statistics_step(n - 1)
+            add(n)
+            send_step(n - 1)
+            return carry
+
+        add(jnp.int32(0))
+        lax.fori_loop(1, 8, step, 0)
+
+    for core in range(2):
+        pl.when(c == core)(functools.partial(first_pass, core))
+    for i, data in enumerate((part_a, part_b, part_c)):
+        wait_bytes(data.at[1 - c], core_sem.at[1, i])
+    for core in range(2):
+        pl.when(c == 1 - core)(functools.partial(second_pass, core))
     statistics_step(jnp.int32(7))
     send_step(jnp.int32(7))
 
@@ -422,19 +390,19 @@
 
     for xl in range(2):
         stat_in[xl, side] = stat[xl, side]
-        wait_bytes(stat_in.at[xl, 0:7], recv_sem.at[xl, 0])
+        wait_bytes(stat_in.at[xl, 0:7], round_recv.at[xl, 0])
         merge(stat_in.at[xl], part.at[xl])
         for r in range(1, 8):
             copy(xl, 1, part.at[xl], part_in.at[xl, y], y_peer(r))
         part_in[xl, y] = part[xl]
     for xl in range(2):
-        wait_bytes(part_in.at[xl, 0:7], recv_sem.at[xl, 1])
+        wait_bytes(part_in.at[xl, 0:7], round_recv.at[xl, 1])
         merge(part_in.at[xl], more.at[xl])
         for r in range(1, 8):
             copy(xl, 2, more.at[xl], more_in.at[xl, z], z_peer(r))
         more_in[xl, z] = more[xl]
     for xl in range(2):
-        wait_bytes(more_in.at[xl, 0:7], recv_sem.at[xl, 2])
+        wait_bytes(more_in.at[xl, 0:7], round_recv.at[xl, 2])
         most, total, picked = combine(more_in.at[xl])
         top[xl, 0:1, :] = most
         top[xl, 1:2, :] = 1.0 / total
@@ -445,7 +413,7 @@
 
     hot = emb_hot[...].astype(BF16)
     hot = jnp.concatenate([hot, hot, hot], axis=0)
-    wait_bytes(top_in.at[0, 0:7], recv_sem.at[0, 3])
+    wait_bytes(top_in.at[0, 0:7], round_recv.at[0, 3])
     fill_score(0, expo, stat, top_in, targets_ref, score)
 
     def head_step(i, carry):
@@ -461,11 +429,64 @@
         return carry
 
     lax.fori_loop(0, 4, head_step, 0)
-    wait_bytes(top_in.at[1, 0:7], recv_sem.at[1, 3])
+    wait_bytes(top_in.at[1, 0:7], round_recv.at[1, 3])
     loss_ref[...] = top_in[xl_here, z, 2:3, :]
     for xl in range(2):
         for phase, data in enumerate((stat_in, part_in, more_in, top_in)):
-            wait_bytes(data.at[xl, 0:7], send_sem.at[xl, phase])
+            wait_bytes(data.at[xl, 0:7], round_send.at[xl, phase])
+    wait_bytes(a.at[p, q, 0:3], send_sem.at[0])
+    wait_bytes(b.at[q, p, 0:3], send_sem.at[1])
+    wait_bytes(cc.at[x, p, 0:7], send_sem.at[2])
+    wait_bytes(cc.at[x, 0:7], send_sem.at[3])
+    wait_bytes(cc.at[0:3], send_sem.at[4])
+    wait_bytes(a.at[p, 0:7], send_sem.at[5])
+    wait_bytes(b.at[q, 0:7], send_sem.at[6])
+    wait_bytes(a.at[0:7], send_sem.at[7])
+    wait_bytes(b.at[0:7], send_sem.at[8])
+    wait_bytes(emb_out.at[pl.ds(0, SEQ - 1)], emb_sem.at[0])
+    for i, data in enumerate((part_a, part_b, part_c)):
+        wait_bytes(data.at[c], core_sem.at[0, i])
+
+
+def hit_of(targets_ref, xl, z_at):
+    row_start = (lax.axis_index("vocab") * SEQ + lax.axis_index("seq")) * ROWS
+    row_ids = lax.broadcasted_iota(jnp.int32, (ROWS, TOK), 0)
+    return (targets_ref[pl.ds(8 * xl + z_at, 1), :] - row_start) == row_ids
+
+
+def core_features(parts, core, xh, xl, z_at, ys):
+    part_a, part_b, part_c = parts
+    x = 2 * xh + xl
+    if core == 0:
+        return jnp.concatenate([part_a[0, z_at, ys, x], part_b[0, ys, z_at, x], part_c[0, x, z_at, ys]], axis=1)
+    return jnp.concatenate([part_a[1, ys, z_at, x], part_b[1, z_at, ys, x], part_c[1, x, ys, z_at]], axis=1)
+
+
+def features_of(parts, xh, xl, z_at, ys):
+    both = jnp.stack([core_features(parts, core, xh, xl, z_at, ys) for core in range(2)], axis=1)
+    return both.reshape(both.shape[0] * 2 * FEAT, TOK)
+
+
+def combine(ref):
+    most = jnp.max(ref[:, 0:1, :], axis=0)
+    total = jnp.sum(ref[:, 1:2, :] * jnp.exp(ref[:, 0:1, :] - most), axis=0)
+    return most, total, jnp.sum(ref[:, 2:3, :], axis=0)
+
+
+def fill_score(xl, expo, stat, top_in, targets_ref, score):
+    def step(z_at, carry):
+        factor = jnp.exp(stat[xl, z_at, 0:1, :] - top_in[xl, z_at, 0:1, :]) * top_in[xl, z_at, 1:2, :]
+        value = expo[xl, z_at] * factor - hit_of(targets_ref, xl, z_at).astype(F32)
+        score[0:ROWS, pl.ds(pl.multiple_of(z_at * TOK, TOK), TOK)] = value.astype(BF16)
+        return carry
+
+    lax.fori_loop(0, 8, step, 0)
+
+
+def head_block(parts, xl, i, score):
+    xh, ys = lax.div(i, 2), pl.ds(4 * lax.rem(i, 2), 4)
+    features = jnp.concatenate([features_of(parts, xh, xl, z_at, ys) for z_at in range(8)], axis=1)
+    return lax.dot_general(features, score[...], (((1,), (1,)), ((), ())), preferred_element_type=F32)
 
 
 def head_kernel(
@@ -495,54 +516,51 @@
     tile = pltpu.VMEM((2, 8, TOK), F32)
     tiles = pltpu.VMEM((2, 8, 8, TOK), F32)
     targets = targets.reshape(SEQ, TOK)
-    *parts, emb_rows, emb_hot, table, targets = pl.pallas_call(
-        gather_kernel,
+    *parts, targets, expo, stat, top_in, loss, turned = pl.pallas_call(
+        main_kernel,
         out_shape=(
             pltpu.VMEM((2, 8, 8, 4, LEN_A, TOK), BF16),
             pltpu.VMEM((2, 8, 8, 4, LEN_B, TOK), BF16),
             pltpu.VMEM((2, 4, 8, 8, LEN_C, TOK), BF16),
-            pltpu.VMEM((SEQ, D), F32),
-            pltpu.VMEM((SEQ, 256), F32),
-            pltpu.VMEM((ROWS, D), BF16),
             pltpu.VMEM((SEQ, TOK), jnp.int32),
+            pltpu.VMEM((2, 8, ROWS, TOK), F32),
+            tiles,
+            tiles,
+            pltpu.VMEM((1, TOK), F32),
+            pltpu.VMEM((4, D // 4, 256), F32),
         ),
         in_specs=[any_space] * 5,
-        out_specs=(vmem,) * 7,
+        out_specs=(vmem,) * 9,
         scratch_shapes=[
+            pltpu.VMEM((ROWS, D), BF16),
+            pltpu.VMEM((2, ROWS, HALF), BF16),
             pltpu.VMEM((1, TOK), jnp.int32),
             pltpu.VMEM((TOK, D), BF16),
             pltpu.VMEM((SEQ, 1, EXTRA), F32),
             pltpu.VMEM((SEQ, 1, EXTRA), F32),
+            pltpu.VMEM((SEQ, D), F32),
+            pltpu.VMEM((SEQ, 256), F32),
+            tiles, tile, tiles, tile, tiles, tile,
+            pltpu.VMEM((256, 8 * TOK), BF16),
             dma((len(ORDER),)),
             dma((len(PHASES),)),
             dma((2, 3)),
             dma((2,)),
             dma((7,)),
+            dma((2, 4)),
+            dma((2, 4)),
         ],
-        compiler_params=pltpu.CompilerParams(collective_id=0, has_side_effects=True, vmem_limit_bytes=47 * 2**20),
-        name="gather",
+        compiler_params=pltpu.CompilerParams(collective_id=0, has_side_effects=True, vmem_limit_bytes=41 * 2**20),
+        cost_estimate=pl.CostEstimate(flops=3 * 2048 * ROWS * D, bytes_accessed=2**22, transcendentals=2048 * ROWS),
+        name="main",
     )(hidden.T, token_ids.reshape(1, TOK), input_grad, table, targets)
-    expo, stat, top_in, loss, turned = pl.pallas_call(
-        logits_kernel,
-        out_shape=(
-            pltpu.VMEM((2, 8, ROWS, TOK), F32), tiles, tiles, pltpu.VMEM((1, TOK), F32), pltpu.VMEM((4, D // 4, 256), F32),
-        ),
-        in_specs=[vmem] * 7,
-        out_specs=(vmem,) * 5,
-        scratch_shapes=[
-            tiles, tile, tiles, tile, tiles, tile, pltpu.VMEM((256, 8 * TOK), BF16), dma((2, 4)), dma((2, 4)),
-        ],
-        compiler_params=pltpu.CompilerParams(collective_id=1, has_side_effects=True, vmem_limit_bytes=24 * 2**20),
-        cost_estimate=pl.CostEstimate(flops=2 * 2048 * ROWS * D, bytes_accessed=2**21, transcendentals=2048 * ROWS),
-        name="logits",
-    )(*parts, table, targets, emb_rows, emb_hot)
     loss, table_grad = pl.pallas_call(
         head_kernel,
         out_shape=(jax.ShapeDtypeStruct((1, TOK), F32), jax.ShapeDtypeStruct((ROWS, D), BF16)),
         in_specs=[vmem] * 9,
         out_specs=(vmem, any_space),
         scratch_shapes=[pltpu.VMEM((256, 8 * TOK), BF16), pltpu.VMEM((ROWS, D), BF16), dma],
-        compiler_params=pltpu.CompilerParams(vmem_limit_bytes=24 * 2**20),
+        compiler_params=pltpu.CompilerParams(vmem_limit_bytes=14 * 2**20),
         cost_estimate=pl.CostEstimate(flops=2 * 2048 * ROWS * D, bytes_accessed=2**21, transcendentals=2048 * ROWS),
         name="head",
     )(*parts, expo, stat, top_in, targets, turned, loss)

time: 93.1 us -> 91.3 us (0.981)
  Pallas kernels: 92.3 us -> 90.5 us
    pallas_call x2 -> x1, Pallas kernels: 87.7 us -> 85.9 us  [on_device(): pl.pallas_call(main_kernel, out_shape=(pltpu.VMEM((2, 8, 8, 4, LEN_A, TOK...]
where the time goes in v4:
time: 91.3 us; the launch traced here: 91.1 us
  Pallas kernels  90.5 us (99%)
    pallas_call x1, Pallas kernels, on_device(): pl.pallas_call(main_kernel, out_shape=(pltpu.VMEM((2, 8, 8, 4, LEN_A, TOK...  85.9 us
    pallas_call x1, Pallas kernels, on_device(): pl.pallas_call(head_kernel, out_shape=(jax.ShapeDtypeStruct((1, TOK), F32...  4.59 us

profile of v4, /device:TPU:1, one launch (start us, length us, event | category | flops | bytes accessed | tf_op | source)
XLA Modules:
  0.0 91.1 jit_solution(5550854929308581589)
XLA Ops:
  0.6 85.9 %main.1 = (bf16[2,8,8,4,32,128]{5,4,3,2,1,0:T(8,128)(2,1)S(1)}, bf16[2,8,8,4,32,128]{5,4,3,2,1,0:T(8,128)(2,1)S(1)}, bf16[2,4,8,8,48,128]{5,4,3,2,1,0:T(8,128)(2...) custom-call(bf16[112,128]{1,0:T(8,128)(2,1)} %bitcast.4, ...), custom_call_target="tpu_custom_call" | custom-call | flops 5505024000 | bytes 4194304 | tf_op jit(solution)/shard_map/main/pallas_call | solution.py:519
  86.5 4.6 %head.1 = (f32[1,128]{1,0:T(1,128)}, bf16[250,3584]{1,0:T(8,128)(2,1)}) custom-call(bf16[2,8,8,4,32,128]{5,4,3,2,1,0:T(8,128)(2,1)S(1)} %get-tuple-element.13.part_a, bf16[2,8,8,4,32,128]{5,4,3,2,1,0:T(8,128)(2,1)S(1)} %get-tuple-element.14.part_b, bf16[2,4,8,8,48,128]{5,4,3,2,1,0:T(8,128)(2,1)S(1)} %get-tuple-element.15.part_c, ...), custom_call_target="tpu_custom_call" | custom-call | flops 3670016000 | bytes 2097152 | tf_op jit(solution)/shard_map/head/pallas_call | solution.py:557

commit v5 on v4

--- a/solution.py
+++ b/solution.py
@@ -149,6 +149,21 @@
     def turn(at, by, length):
         return lax.rem(at + (by + length), length) if by else at
 
+    xh, xl_here = lax.div(x, 2), lax.rem(x, 2)
+    side = 2 * x + c
+
+    def z_peer(r):
+        return (v, xl_here * 8 + lax.rem(z + r, 8))
+
+    def y_peer(r):
+        return (xh * 16 + lax.rem(y + r, 8) * 2 + c, s)
+
+    def x_peer(r):
+        other = lax.rem(side + r, 8)
+        x_at = lax.div(other, 2)
+        return (lax.div(x_at, 2) * 16 + y * 2 + lax.rem(other, 2), lax.rem(x_at, 2) * 8 + z)
+
+    x_peers, y_peers, z_peers = ([peer(r) for r in range(1, 8)] for peer in (x_peer, y_peer, z_peer))
     sibling = (v + 1 - 2 * c, s)
     a, b, cc = part_a.at[c], part_b.at[c], part_c.at[c]
 
@@ -163,6 +178,7 @@
     table_copy = pltpu.make_async_copy(table_ref, table_v, local_sem.at[6])
     for copy in own:
         copy.start()
+    table_copy.start()
 
     partners = [device(turn(x, d, 4), p, q) for d in (1, -1, 2)]
     partners += [device(x, turn(p, d, 8), q) for d in (1, -1, 2, -2)]
@@ -171,8 +187,24 @@
     barrier = pltpu.get_barrier_semaphore()
     for partner in partners:
         pl.semaphore_signal(barrier, inc=1, device_id=partner, device_id_type=MESH)
-    for copy in (ids_copy, grad_copy, targets_copy, table_copy):
+    for copy in (ids_copy, grad_copy, targets_copy):
         copy.start()
+
+    def split_columns(core, j):
+        n0 = 256 * j
+        low = (n0 + FEAT * (n0 // FEAT) + FEAT * core) // 128 * 128
+        width = min(768, D - low)
+        n = lax.broadcasted_iota(jnp.int32, (width, 256), 1) + n0
+        chunk = sum((n >= FEAT * k).astype(jnp.int32) for k in range(n0 // FEAT + 1, (n0 + 255) // FEAT + 1))
+        source = n + FEAT * (chunk + n0 // FEAT + core) - low
+        pick = (lax.broadcasted_iota(jnp.int32, (width, 256), 0) == source).astype(F32).astype(BF16)
+        columns = jnp.dot(table_v[:, low : low + width], pick, preferred_element_type=F32)
+        table_c[core, :, n0 : n0 + 256] = columns.astype(BF16)
+
+    splits = [(core, j) for core in range(2) for j in range(HALF // 256)]
+    table_copy.wait()
+    for core, j in splits[:8]:
+        split_columns(core, j)
     for copy in own:
         copy.wait()
     pl.semaphore_wait(barrier, len(partners))
@@ -249,15 +281,12 @@
             emb_out[j, :, D:EXTRA] = tail[j : j + 1, :]
         emb_in[s] = emb_out[s]
 
-        def send_row(r, carry):
-            j = lax.rem(s + r, SEQ)
-            pltpu.make_async_remote_copy(
-                src_ref=emb_out.at[j], dst_ref=emb_in.at[s], send_sem=emb_sem.at[0], recv_sem=emb_sem.at[1],
-                device_id=(v, j), device_id_type=MESH,
-            ).start()
-            return carry
-
-        lax.fori_loop(1, SEQ, send_row, 0)
+    def send_row(r):
+        j = lax.rem(s + r, SEQ)
+        pltpu.make_async_remote_copy(
+            src_ref=emb_out.at[j], dst_ref=emb_in.at[s], send_sem=emb_sem.at[0], recv_sem=emb_sem.at[1],
+            device_id=(v, j), device_id_type=MESH,
+        ).start()
 
     def embed_arrived():
         wait_bytes(emb_in.at[pl.ds(0, SEQ - 1)], emb_sem.at[1])
@@ -266,50 +295,20 @@
             emb_rows[j : j + 1, :] = emb_in[j, :, 0:D]
             emb_hot[j : j + 1, :] = (lane_ids == emb_in[j, :, D : D + 1]).astype(F32)
 
-    def split_columns(core, j):
-        n0 = 256 * j
-        low = (n0 + FEAT * (n0 // FEAT) + FEAT * core) // 128 * 128
-        width = min(768, D - low)
-        n = lax.broadcasted_iota(jnp.int32, (width, 256), 1) + n0
-        chunk = sum((n >= FEAT * k).astype(jnp.int32) for k in range(n0 // FEAT + 1, (n0 + 255) // FEAT + 1))
-        source = n + FEAT * (chunk + n0 // FEAT + core) - low
-        pick = (lax.broadcasted_iota(jnp.int32, (width, 256), 0) == source).astype(F32).astype(BF16)
-        columns = jnp.dot(table_v[:, low : low + width], pick, preferred_element_type=F32)
-        table_c[core, :, n0 : n0 + 256] = columns.astype(BF16)
-
-    splits = [(core, j) for core in range(2) for j in range(HALF // 256)]
+    needed = {key for key in MESSAGES if key[0] in ("XA", "XB", "AQ", "BP")}
+    middle = max(36, 1 + max(ORDER.index(key) for key in needed))
+    others = [functools.partial(split_columns, *split) for split in splits[8:]]
+    others += [embed_rows] + [functools.partial(send_row, r) for r in range(1, SEQ)]
     send_ready()
-    embedded = False
-    needed = {key for key in MESSAGES if key[0] in ("XA", "XB", "AQ", "BP")}
-    for key in ORDER:
+    for i, key in enumerate(ORDER):
         wait_bytes(arrived(key), recv_sem.at[RECV[key]])
         done.add(key)
         send_ready()
-        if not embedded and needed <= done:
-            embedded = True
-            embed_rows()
-        if len(done) == 20:
-            table_copy.wait()
-        if len(done) > 20 and splits:
-            split_columns(*splits.pop(0))
-        if len(done) == len(ORDER) * 4 // 5:
-            embed_arrived()
+        if i >= middle and others:
+            others.pop(0)()
+    assert not others
 
     targets_copy.wait()
-    xh, xl_here = lax.div(x, 2), lax.rem(x, 2)
-    side = 2 * x + c
-
-    def z_peer(r):
-        return (v, xl_here * 8 + lax.rem(z + r, 8))
-
-    def y_peer(r):
-        return (xh * 16 + lax.rem(y + r, 8) * 2 + c, s)
-
-    def x_peer(r):
-        other = lax.rem(side + r, 8)
-        x = lax.div(other, 2)
-        return (lax.div(x, 2) * 16 + y * 2 + lax.rem(other, 2), lax.rem(x, 2) * 8 + z)
-
     def copy(xl, phase, data, into, peer):
         pltpu.make_async_remote_copy(
             src_ref=data, dst_ref=into, send_sem=round_send.at[xl, phase], recv_sem=round_recv.at[xl, phase],
@@ -393,14 +392,15 @@
         wait_bytes(stat_in.at[xl, 0:7], round_recv.at[xl, 0])
         merge(stat_in.at[xl], part.at[xl])
         for r in range(1, 8):
-            copy(xl, 1, part.at[xl], part_in.at[xl, y], y_peer(r))
+            copy(xl, 1, part.at[xl], part_in.at[xl, y], y_peers[r - 1])
         part_in[xl, y] = part[xl]
     for xl in range(2):
         wait_bytes(part_in.at[xl, 0:7], round_recv.at[xl, 1])
         merge(part_in.at[xl], more.at[xl])
         for r in range(1, 8):
-            copy(xl, 2, more.at[xl], more_in.at[xl, z], z_peer(r))
+            copy(xl, 2, more.at[xl], more_in.at[xl, z], z_peers[r - 1])
         more_in[xl, z] = more[xl]
+    embed_arrived()
     for xl in range(2):
         wait_bytes(more_in.at[xl, 0:7], round_recv.at[xl, 2])
         most, total, picked = combine(more_in.at[xl])
@@ -408,7 +408,7 @@
         top[xl, 1:2, :] = 1.0 / total
         top[xl, 2:3, :] = most + jnp.log(total) - picked
         for r in range(1, 8):
-            copy(xl, 3, top.at[xl], top_in.at[xl, side], x_peer(r))
+            copy(xl, 3, top.at[xl], top_in.at[xl, side], x_peers[r - 1])
         top_in[xl, side] = top[xl]
 
     hot = emb_hot[...].astype(BF16)
@@ -416,9 +416,8 @@
     wait_bytes(top_in.at[0, 0:7], round_recv.at[0, 3])
     fill_score(0, expo, stat, top_in, targets_ref, score)
 
-    def head_step(i, carry):
-        at = pl.ds(pl.multiple_of(i * (D // 4), 128), D // 4)
-        rest = emb_rows[:, at]
+    for i in range(4):
+        rest = emb_rows[:, i * (D // 4) : (i + 1) * (D // 4)]
         high = rest.astype(BF16)
         rest = rest - high.astype(F32)
         middle = rest.astype(BF16)
@@ -426,9 +425,6 @@
         terms = jnp.concatenate([high, middle, low], axis=0)
         embed = lax.dot_general(terms, hot, (((0,), (0,)), ((), ())), preferred_element_type=F32)
         turned[i] = head_block(parts, 0, i, score) + embed
-        return carry
-
-    lax.fori_loop(0, 4, head_step, 0)
     wait_bytes(top_in.at[1, 0:7], round_recv.at[1, 3])
     loss_ref[...] = top_in[xl_here, z, 2:3, :]
     for xl in range(2):
@@ -484,7 +480,7 @@
 
 
 def head_block(parts, xl, i, score):
-    xh, ys = lax.div(i, 2), pl.ds(4 * lax.rem(i, 2), 4)
+    xh, ys = i // 2, slice(4 * (i % 2), 4 * (i % 2) + 4)
     features = jnp.concatenate([features_of(parts, xh, xl, z_at, ys) for z_at in range(8)], axis=1)
     return lax.dot_general(features, score[...], (((1,), (1,)), ((), ())), preferred_element_type=F32)
 
@@ -498,14 +494,14 @@
     loss_ref[...] = loss_in[...]
     fill_score(1, expo, stat, top_in, targets_ref, score)
 
-    def head_step(i, carry):
-        at = pl.ds(pl.multiple_of(i * (D // 4), 128), D // 4)
-        total = jnp.transpose(turned[i] + head_block(parts, 1, i, score))
-        out_v[:, at] = total[0:ROWS, :].astype(BF16)
-        pltpu.make_async_copy(out_v.at[:, at], out_ref.at[:, at], out_sem).start()
-        return carry
-
-    lax.fori_loop(0, 4, head_step, 0)
+    ready = None
+    for i in range(5):
+        total = (turned[i] + head_block(parts, 1, i, score)).astype(BF16) if i < 4 else None
+        if ready is not None:
+            at = pl.ds((i - 1) * (D // 4), D // 4)
+            out_v[:, at] = jnp.transpose(ready)[0:ROWS, :]
+            pltpu.make_async_copy(out_v.at[:, at], out_ref.at[:, at], out_sem).start()
+        ready = total
     pltpu.make_async_copy(out_v, out_ref, out_sem).wait()
 
 

time: 91.3 us -> 89 us (0.975)
  Pallas kernels: 90.5 us -> 88.2 us
    pallas_call x1, Pallas kernels: 85.9 us -> 84.2 us  [on_device(): pl.pallas_call(main_kernel, out_shape=(pltpu.VMEM((2, 8, 8, 4, LEN_A, TOK...]
where the time goes in v5:
time: 89 us; the launch traced here: 88.8 us
  Pallas kernels  88.2 us (99%)
    pallas_call x1, Pallas kernels, on_device(): pl.pallas_call(main_kernel, out_shape=(pltpu.VMEM((2, 8, 8, 4, LEN_A, TOK...  84.2 us
    pallas_call x1, Pallas kernels, on_device(): pl.pallas_call(head_kernel, out_shape=(jax.ShapeDtypeStruct((1, TOK), F32...  3.97 us

profile of v5, /device:TPU:1, one launch (start us, length us, event | category | flops | bytes accessed | tf_op | source)
XLA Modules:
  0.0 88.8 jit_solution(8217399225139713294)
XLA Ops:
  0.6 84.2 %main.1 = (bf16[2,8,8,4,32,128]{5,4,3,2,1,0:T(8,128)(2,1)S(1)}, bf16[2,8,8,4,32,128]{5,4,3,2,1,0:T(8,128)(2,1)S(1)}, bf16[2,4,8,8,48,128]{5,4,3,2,1,0:T(8,128)(2...) custom-call(bf16[112,128]{1,0:T(8,128)(2,1)} %bitcast.4, ...), custom_call_target="tpu_custom_call" | custom-call | flops 5505024000 | bytes 4194304 | tf_op jit(solution)/shard_map/main/pallas_call | solution.py:515
  84.9 4.0 %head.1 = (f32[1,128]{1,0:T(1,128)}, bf16[250,3584]{1,0:T(8,128)(2,1)}) custom-call(bf16[2,8,8,4,32,128]{5,4,3,2,1,0:T(8,128)(2,1)S(1)} %get-tuple-element.13.part_a, bf16[2,8,8,4,32,128]{5,4,3,2,1,0:T(8,128)(2,1)S(1)} %get-tuple-element.14.part_b, bf16[2,4,8,8,48,128]{5,4,3,2,1,0:T(8,128)(2,1)S(1)} %get-tuple-element.15.part_c, ...), custom_call_target="tpu_custom_call" | custom-call | flops 3670016000 | bytes 2097152 | tf_op jit(solution)/shard_map/head/pallas_call | solution.py:553

commit v6 on v5

--- a/solution.py
+++ b/solution.py
@@ -127,9 +127,9 @@
 
 def main_kernel(
     hidden_ref, ids_hbm, input_grad_ref, table_ref, targets_hbm,
-    part_a, part_b, part_c, targets_ref, expo, stat, top_in, loss_ref, turned,
+    part_a, part_b, part_c, targets_ref, expo, most, lse, loss_ref, turned,
     table_v, table_c, ids_ref, grad_v, emb_out, emb_in, emb_rows, emb_hot,
-    stat_in, part, part_in, more, more_in, top, score,
+    lse_out, lse_in, pick_out, pick_in, score,
     recv_sem, send_sem, core_sem, emb_sem, local_sem, round_send, round_recv,
 ):
     parts = (part_a, part_b, part_c)
@@ -194,7 +194,7 @@
         n0 = 256 * j
         low = (n0 + FEAT * (n0 // FEAT) + FEAT * core) // 128 * 128
         width = min(768, D - low)
-        n = lax.broadcasted_iota(jnp.int32, (width, 256), 1) + n0
+        n = lax.broadcasted_iota(jnp.int32, (1, 256), 1) + n0
         chunk = sum((n >= FEAT * k).astype(jnp.int32) for k in range(n0 // FEAT + 1, (n0 + 255) // FEAT + 1))
         source = n + FEAT * (chunk + n0 // FEAT + core) - low
         pick = (lax.broadcasted_iota(jnp.int32, (width, 256), 0) == source).astype(F32).astype(BF16)
@@ -309,18 +309,11 @@
     assert not others
 
     targets_copy.wait()
-    def copy(xl, phase, data, into, peer):
-        pltpu.make_async_remote_copy(
-            src_ref=data, dst_ref=into, send_sem=round_send.at[xl, phase], recv_sem=round_recv.at[xl, phase],
-            device_id=peer, device_id_type=MESH,
-        ).start()
-
     def blocks_of(n):
-        xl, m = lax.div(n, 4), lax.rem(n, 4)
-        return xl, m, [lax.rem(side + 1 + 2 * m + k, 8) for k in range(2)]
+        return lax.div(n, 4), [2 * lax.rem(n, 4) + k for k in range(2)]
 
     def logits_step(n, core):
-        xl, _, blocks = blocks_of(n)
+        xl, blocks = blocks_of(n)
         columns = [
             jnp.concatenate([core_features(parts, core, half, xl, z_at, slice(None)).reshape(HALF // 2, TOK) for half in range(2)], axis=0)
             for z_at in blocks
@@ -329,24 +322,40 @@
         return xl, [(z_at, values[:, k * TOK : (k + 1) * TOK]) for k, z_at in enumerate(blocks)]
 
     def statistics_step(n):
-        xl, _, blocks = blocks_of(n)
+        xl, blocks = blocks_of(n)
         for z_at in blocks:
             values = expo[xl, z_at]
-            most = jnp.max(values, axis=0, keepdims=True)
-            above = jnp.exp(values - most)
-            stat[xl, z_at, 0:1, :] = most
-            stat[xl, z_at, 1:2, :] = jnp.sum(above, axis=0, keepdims=True)
+            top = jnp.max(values, axis=0, keepdims=True)
+            above = jnp.exp(values - top)
+            most[xl, pl.ds(z_at, 1), :] = top
+            lse_out[xl, 0, pl.ds(z_at, 1), :] = top + jnp.log(jnp.sum(above, axis=0, keepdims=True))
             hit = hit_of(targets_ref, xl, z_at)
-            stat[xl, z_at, 2:3, :] = jnp.sum(jnp.where(hit, values, 0.0), axis=0, keepdims=True)
+            pick_out[0, pl.ds(8 * xl + z_at, 1), :] = jnp.sum(jnp.where(hit, values, 0.0), axis=0, keepdims=True)
             expo[xl, z_at] = above
 
-    def send_step(n):
-        xl, m, blocks = blocks_of(n)
-        copy(xl, 0, stat.at[xl, blocks[0]], stat_in.at[xl, side], x_peer(1 + 2 * m))
-
-        @pl.when(m < 3)
-        def _():
-            copy(xl, 0, stat.at[xl, blocks[1]], stat_in.at[xl, side], x_peer(2 + 2 * m))
+    def round_refs(stream, step):
+        if stream < 2:
+            return lse_out.at[stream, step], lse_in.at[stream, step]
+        return pick_out.at[step], pick_in.at[step]
+
+    def send_round(stream, step):
+        data, into = round_refs(stream, step)
+        here = (side, y, z)[step]
+        for peer in (x_peers, y_peers, z_peers)[step]:
+            pltpu.make_async_remote_copy(
+                src_ref=data, dst_ref=into.at[here], send_sem=round_send.at[stream, step], recv_sem=round_recv.at[stream, step],
+                device_id=peer, device_id_type=MESH,
+            ).start()
+        into[here] = data[...]
+
+    def merged(stream, step):
+        _, into = round_refs(stream, step)
+        wait_bytes(into.at[0:7], round_recv.at[stream, step])
+        values = into[...]
+        if stream == 2:
+            return jnp.sum(values, axis=0)
+        top = jnp.max(values, axis=0)
+        return top + jnp.log(jnp.sum(jnp.exp(values - top), axis=0))
 
     def first_pass(core):
         def step(n, carry):
@@ -366,11 +375,12 @@
         def step(n, carry):
             statistics_step(n - 1)
             add(n)
-            send_step(n - 1)
             return carry
 
         add(jnp.int32(0))
-        lax.fori_loop(1, 8, step, 0)
+        lax.fori_loop(1, 5, step, 0)
+        send_round(0, 0)
+        lax.fori_loop(5, 8, step, 0)
 
     for core in range(2):
         pl.when(c == core)(functools.partial(first_pass, core))
@@ -379,42 +389,19 @@
     for core in range(2):
         pl.when(c == 1 - core)(functools.partial(second_pass, core))
     statistics_step(jnp.int32(7))
-    send_step(jnp.int32(7))
-
-    def merge(source, into):
-        most, total, picked = combine(source)
-        into[0:1, :] = most
-        into[1:2, :] = total
-        into[2:3, :] = picked
-
-    for xl in range(2):
-        stat_in[xl, side] = stat[xl, side]
-        wait_bytes(stat_in.at[xl, 0:7], round_recv.at[xl, 0])
-        merge(stat_in.at[xl], part.at[xl])
-        for r in range(1, 8):
-            copy(xl, 1, part.at[xl], part_in.at[xl, y], y_peers[r - 1])
-        part_in[xl, y] = part[xl]
-    for xl in range(2):
-        wait_bytes(part_in.at[xl, 0:7], round_recv.at[xl, 1])
-        merge(part_in.at[xl], more.at[xl])
-        for r in range(1, 8):
-            copy(xl, 2, more.at[xl], more_in.at[xl, z], z_peers[r - 1])
-        more_in[xl, z] = more[xl]
+    send_round(1, 0)
+    send_round(2, 0)
+    for step in range(2):
+        for stream in range(3):
+            data, _ = round_refs(stream, step + 1)
+            data[...] = merged(stream, step)
+            send_round(stream, step + 1)
     embed_arrived()
-    for xl in range(2):
-        wait_bytes(more_in.at[xl, 0:7], round_recv.at[xl, 2])
-        most, total, picked = combine(more_in.at[xl])
-        top[xl, 0:1, :] = most
-        top[xl, 1:2, :] = 1.0 / total
-        top[xl, 2:3, :] = most + jnp.log(total) - picked
-        for r in range(1, 8):
-            copy(xl, 3, top.at[xl], top_in.at[xl, side], x_peers[r - 1])
-        top_in[xl, side] = top[xl]
 
     hot = emb_hot[...].astype(BF16)
     hot = jnp.concatenate([hot, hot, hot], axis=0)
-    wait_bytes(top_in.at[0, 0:7], round_recv.at[0, 3])
-    fill_score(0, expo, stat, top_in, targets_ref, score)
+    lse[0] = merged(0, 2)
+    fill_score(0, expo, most, lse, targets_ref, score)
 
     for i in range(4):
         rest = emb_rows[:, i * (D // 4) : (i + 1) * (D // 4)]
@@ -425,11 +412,12 @@
         terms = jnp.concatenate([high, middle, low], axis=0)
         embed = lax.dot_general(terms, hot, (((0,), (0,)), ((), ())), preferred_element_type=F32)
         turned[i] = head_block(parts, 0, i, score) + embed
-    wait_bytes(top_in.at[1, 0:7], round_recv.at[1, 3])
-    loss_ref[...] = top_in[xl_here, z, 2:3, :]
-    for xl in range(2):
-        for phase, data in enumerate((stat_in, part_in, more_in, top_in)):
-            wait_bytes(data.at[xl, 0:7], round_send.at[xl, phase])
+    lse[1] = merged(1, 2)
+    pick_out[3] = merged(2, 2)
+    loss_ref[...] = lse[xl_here, pl.ds(z, 1), :] - pick_out[3, pl.ds(8 * xl_here + z, 1), :]
+    for stream in range(3):
+        for step in range(3):
+            wait_bytes(round_refs(stream, step)[1].at[0:7], round_send.at[stream, step])
     wait_bytes(a.at[p, q, 0:3], send_sem.at[0])
     wait_bytes(b.at[q, p, 0:3], send_sem.at[1])
     wait_bytes(cc.at[x, p, 0:7], send_sem.at[2])
@@ -463,15 +451,9 @@
     return both.reshape(both.shape[0] * 2 * FEAT, TOK)
 
 
-def combine(ref):
-    most = jnp.max(ref[:, 0:1, :], axis=0)
-    total = jnp.sum(ref[:, 1:2, :] * jnp.exp(ref[:, 0:1, :] - most), axis=0)
-    return most, total, jnp.sum(ref[:, 2:3, :], axis=0)
-
-
-def fill_score(xl, expo, stat, top_in, targets_ref, score):
+def fill_score(xl, expo, most, lse, targets_ref, score):
     def step(z_at, carry):
-        factor = jnp.exp(stat[xl, z_at, 0:1, :] - top_in[xl, z_at, 0:1, :]) * top_in[xl, z_at, 1:2, :]
+        factor = jnp.exp(most[xl, pl.ds(z_at, 1), :] - lse[xl, pl.ds(z_at, 1), :])
         value = expo[xl, z_at] * factor - hit_of(targets_ref, xl, z_at).astype(F32)
         score[0:ROWS, pl.ds(pl.multiple_of(z_at * TOK, TOK), TOK)] = value.astype(BF16)
         return carry
@@ -486,13 +468,13 @@
 
 
 def head_kernel(
-    part_a, part_b, part_c, expo, stat, top_in, targets_ref, turned, loss_in,
+    part_a, part_b, part_c, expo, most, lse, targets_ref, turned, loss_in,
     loss_ref, out_ref,
     score, out_v, out_sem,
 ):
     parts = (part_a, part_b, part_c)
     loss_ref[...] = loss_in[...]
-    fill_score(1, expo, stat, top_in, targets_ref, score)
+    fill_score(1, expo, most, lse, targets_ref, score)
 
     ready = None
     for i in range(5):
@@ -509,10 +491,9 @@
     any_space = pl.BlockSpec(memory_space=pl.ANY)
     vmem = pl.BlockSpec(memory_space=pltpu.VMEM)
     dma = pltpu.SemaphoreType.DMA
-    tile = pltpu.VMEM((2, 8, TOK), F32)
-    tiles = pltpu.VMEM((2, 8, 8, TOK), F32)
+    tiles = pltpu.VMEM((2, 8, TOK), F32)
     targets = targets.reshape(SEQ, TOK)
-    *parts, targets, expo, stat, top_in, loss, turned = pl.pallas_call(
+    *parts, targets, expo, most, lse, loss, turned = pl.pallas_call(
         main_kernel,
         out_shape=(
             pltpu.VMEM((2, 8, 8, 4, LEN_A, TOK), BF16),
@@ -536,15 +517,18 @@
             pltpu.VMEM((SEQ, 1, EXTRA), F32),
             pltpu.VMEM((SEQ, D), F32),
             pltpu.VMEM((SEQ, 256), F32),
-            tiles, tile, tiles, tile, tiles, tile,
+            pltpu.VMEM((2, 3, 8, TOK), F32),
+            pltpu.VMEM((2, 3, 8, 8, TOK), F32),
+            pltpu.VMEM((4, SEQ, TOK), F32),
+            pltpu.VMEM((3, 8, SEQ, TOK), F32),
             pltpu.VMEM((256, 8 * TOK), BF16),
             dma((len(ORDER),)),
             dma((len(PHASES),)),
             dma((2, 3)),
             dma((2,)),
             dma((7,)),
-            dma((2, 4)),
-            dma((2, 4)),
+            dma((3, 3)),
+            dma((3, 3)),
         ],
         compiler_params=pltpu.CompilerParams(collective_id=0, has_side_effects=True, vmem_limit_bytes=41 * 2**20),
         cost_estimate=pl.CostEstimate(flops=3 * 2048 * ROWS * D, bytes_accessed=2**22, transcendentals=2048 * ROWS),
@@ -559,7 +543,7 @@
         compiler_params=pltpu.CompilerParams(vmem_limit_bytes=14 * 2**20),
         cost_estimate=pl.CostEstimate(flops=2 * 2048 * ROWS * D, bytes_accessed=2**21, transcendentals=2048 * ROWS),
         name="head",
-    )(*parts, expo, stat, top_in, targets, turned, loss)
+    )(*parts, expo, most, lse, targets, turned, loss)
     return loss.reshape(TOK), table_grad
 
 

time: 89 us -> 84.5 us (0.949)
  Pallas kernels: 88.2 us -> 83.7 us
    pallas_call x1, Pallas kernels: 84.2 us -> 79.7 us  [on_device(): pl.pallas_call(main_kernel, out_shape=(pltpu.VMEM((2, 8, 8, 4, LEN_A, TOK...]
where the time goes in v6:
time: 84.5 us; the launch traced here: 84.3 us
  Pallas kernels  83.7 us (99%)
    pallas_call x1, Pallas kernels, on_device(): pl.pallas_call(main_kernel, out_shape=(pltpu.VMEM((2, 8, 8, 4, LEN_A, TOK...  79.7 us
    pallas_call x1, Pallas kernels, on_device(): pl.pallas_call(head_kernel, out_shape=(jax.ShapeDtypeStruct((1, TOK), F32...  3.96 us

profile of v6, /device:TPU:1, one launch (start us, length us, event | category | flops | bytes accessed | tf_op | source)
XLA Modules:
  0.0 84.3 jit_solution(13117686941499983104)
XLA Ops:
  0.6 79.7 %main.1 = (bf16[2,8,8,4,32,128]{5,4,3,2,1,0:T(8,128)(2,1)S(1)}, bf16[2,8,8,4,32,128]{5,4,3,2,1,0:T(8,128)(2,1)S(1)}, bf16[2,4,8,8,48,128]{5,4,3,2,1,0:T(8,128)(2...) custom-call(bf16[112,128]{1,0:T(8,128)(2,1)} %bitcast.4, ...), custom_call_target="tpu_custom_call" | custom-call | flops 5505024000 | bytes 4194304 | tf_op jit(solution)/shard_map/main/pallas_call | solution.py:496
  80.4 4.0 %head.1 = (f32[1,128]{1,0:T(1,128)}, bf16[250,3584]{1,0:T(8,128)(2,1)}) custom-call(bf16[2,8,8,4,32,128]{5,4,3,2,1,0:T(8,128)(2,1)S(1)} %get-tuple-element.13.part_a, bf16[2,8,8,4,32,128]{5,4,3,2,1,0:T(8,128)(2,1)S(1)} %get-tuple-element.14.part_b, bf16[2,4,8,8,48,128]{5,4,3,2,1,0:T(8,128)(2,1)S(1)} %get-tuple-element.15.part_c, ...), custom_call_target="tpu_custom_call" | custom-call | flops 3670016000 | bytes 2097152 | tf_op jit(solution)/shard_map/head/pallas_call | solution.py:537

commit v7 on v6

--- a/solution.py
+++ b/solution.py
@@ -21,7 +21,7 @@
 HALF = D // 2
 EXTRA = D + 128
 LEN_A, LEN_B, LEN_C = 32, 32, 48
-GROUP = 4
+GROUP = 2
 PAIR = 1
 
 
@@ -35,11 +35,11 @@
         for rel in rels:
             put((name, 0, 1 if rel > 0 else -1, abs(rel)), size, axis, abs(rel), [])
 
-    def ring(name, unit, axis, size, length, deps, flip, stride=1):
+    def ring(name, unit, axis, size, length, deps, flip, hops_of=(1, 1, 1, 1)):
         far = (length // 2, length // 2 - 1)
         for step, most in zip((1, -1), far[::-1] if flip else far):
             for dist in range(1, most + 1):
-                hops = (dist - 1) % stride + 1
+                hops = hops_of[dist - 1]
                 put((name, unit, step, dist), size, axis, hops, deps if dist == hops else [(name, unit, step, dist - hops)])
 
     def item(name, rel, flip):
@@ -60,12 +60,12 @@
     direct("CQ", "q", LEN_C, (1, -1, 2, -2, 3, -3, 4))
     direct("XA", "x", LEN_A, (1, -1, 2))
     direct("XB", "x", LEN_B, (1, -1, 2))
-    ring("CP", 0, "p", 8 * LEN_C, 8, of("CQ"), False)
+    ring("CP", 0, "p", 8 * LEN_C, 8, of("CQ"), False, (1, 2, 1, 1))
     for unit, rels in whole[PAIR].items():
         deps = of("CQ") + [key for rel in rels for key in item("CP", rel, False)]
         ring("CX", unit, "x", PAIR * 8 * LEN_C, 4, deps, unit % 2 == 1)
-    ring("AQ", 0, "q", 4 * LEN_A, 8, of("XA"), False, 2)
-    ring("BP", 0, "p", 4 * LEN_B, 8, of("XB"), True, 2)
+    ring("AQ", 0, "q", 4 * LEN_A, 8, of("XA"), False, (1, 2, 1, 2))
+    ring("BP", 0, "p", 4 * LEN_B, 8, of("XB"), True, (1, 2, 1, 2))
     for name, axis, first, source, flip, size in (("AP", "p", "XA", "AQ", False, LEN_A), ("BQ", "q", "XB", "BP", True, LEN_B)):
         for unit, rels in whole[GROUP].items():
             deps = of(first) + [key for rel in rels for key in item(source, rel, flip)]
@@ -75,7 +75,12 @@
     put(("SC", 0, 0, 0), 64 * LEN_C, "s", 1, of("CQ", "CP"))
     for rel in range(1, 8):
         for name, source, size in (("SA", "AP", LEN_A), ("SB", "BQ", LEN_B)):
-            put((name, rel, 0, 0), 32 * size, "s", 1, [k for k in of(source) if (-k[2] * k[3]) % 8 == rel])
+            keys = [key for key in of(source) if (-key[2] * key[3]) % 8 == rel]
+            if rel == 4:
+                for key in keys:
+                    put((name,) + key, messages[key]["size"] // 256, "s", 1, [key])
+            else:
+                put((name, rel, 0, 0), 32 * size, "s", 1, keys)
     for key in of("CX"):
         put(("SC",) + key, PAIR * 8 * LEN_C, "s", 1, [key])
     return messages
@@ -94,7 +99,7 @@
 
     def start(core, key, now):
         m = messages[key]
-        free[core] = now = max(now, free[core]) + 0.05
+        free[core] = now = max(now, free[core]) + 0.1
         lane = ("s", core) if m["axis"] == "s" else (turned[m["axis"]] if core else m["axis"], key[2])
         rate = 6e5 if m["axis"] == "s" else 8.5e4
         link[lane] = max(now, link.get(lane, 0.0)) + m["size"] * m["hops"] / rate
@@ -129,7 +134,7 @@
     hidden_ref, ids_hbm, input_grad_ref, table_ref, targets_hbm,
     part_a, part_b, part_c, targets_ref, expo, most, lse, loss_ref, turned,
     table_v, table_c, ids_ref, grad_v, emb_out, emb_in, emb_rows, emb_hot,
-    lse_out, lse_in, pick_out, pick_in, score,
+    lse_out, lse_in, pick_first, pick_out, pick_in, score,
     recv_sem, send_sem, core_sem, emb_sem, local_sem, round_send, round_recv,
 ):
     parts = (part_a, part_b, part_c)
@@ -164,6 +169,7 @@
         return (lax.div(x_at, 2) * 16 + y * 2 + lax.rem(other, 2), lax.rem(x_at, 2) * 8 + z)
 
     x_peers, y_peers, z_peers = ([peer(r) for r in range(1, 8)] for peer in (x_peer, y_peer, z_peer))
+    z_places = [lax.rem(z + r, 8) for r in range(1, 8)]
     sibling = (v + 1 - 2 * c, s)
     a, b, cc = part_a.at[c], part_b.at[c], part_c.at[c]
 
@@ -214,6 +220,8 @@
 
     def block(key, shift):
         name, unit = key[0], key[1]
+        if isinstance(unit, str):
+            return arrived(key[1:])
         if name == "XA":
             return a.at[p, q, turn(x, shift, 4)]
         if name == "XB":
@@ -236,7 +244,7 @@
             return a.at[turn(p, unit, 8)]
         if name == "SB":
             return b.at[turn(q, unit, 8)]
-        return arrived(key[1:]) if unit else cc.at[x]
+        return cc.at[x]
 
     def arrived(key):
         return block(key, -key[2] * key[3])
@@ -330,23 +338,26 @@
             most[xl, pl.ds(z_at, 1), :] = top
             lse_out[xl, 0, pl.ds(z_at, 1), :] = top + jnp.log(jnp.sum(above, axis=0, keepdims=True))
             hit = hit_of(targets_ref, xl, z_at)
-            pick_out[0, pl.ds(8 * xl + z_at, 1), :] = jnp.sum(jnp.where(hit, values, 0.0), axis=0, keepdims=True)
+            pick_first[z_at, pl.ds(xl, 1), :] = jnp.sum(jnp.where(hit, values, 0.0), axis=0, keepdims=True)
             expo[xl, z_at] = above
 
     def round_refs(stream, step):
         if stream < 2:
             return lse_out.at[stream, step], lse_in.at[stream, step]
-        return pick_out.at[step], pick_in.at[step]
+        return pick_out.at[max(step, 1)], pick_in.at[step]
 
     def send_round(stream, step):
         data, into = round_refs(stream, step)
-        here = (side, y, z)[step]
-        for peer in (x_peers, y_peers, z_peers)[step]:
+        axis = step if stream < 2 else 2 - step
+        here = (side, y, z)[axis]
+        for r, peer in enumerate((x_peers, y_peers, z_peers)[axis]):
+            scatter = stream == 2 and step == 0
             pltpu.make_async_remote_copy(
-                src_ref=data, dst_ref=into.at[here], send_sem=round_send.at[stream, step], recv_sem=round_recv.at[stream, step],
+                src_ref=pick_first.at[z_places[r]] if scatter else data, dst_ref=into.at[here],
+                send_sem=round_send.at[stream, step], recv_sem=round_recv.at[stream, step],
                 device_id=peer, device_id_type=MESH,
             ).start()
-        into[here] = data[...]
+        into[here] = pick_first[z] if stream == 2 and step == 0 else data[...]
 
     def merged(stream, step):
         _, into = round_refs(stream, step)
@@ -413,8 +424,8 @@
         embed = lax.dot_general(terms, hot, (((0,), (0,)), ((), ())), preferred_element_type=F32)
         turned[i] = head_block(parts, 0, i, score) + embed
     lse[1] = merged(1, 2)
-    pick_out[3] = merged(2, 2)
-    loss_ref[...] = lse[xl_here, pl.ds(z, 1), :] - pick_out[3, pl.ds(8 * xl_here + z, 1), :]
+    pick_out[0] = merged(2, 2)
+    loss_ref[...] = lse[xl_here, pl.ds(z, 1), :] - pick_out[0, pl.ds(xl_here, 1), :]
     for stream in range(3):
         for step in range(3):
             wait_bytes(round_refs(stream, step)[1].at[0:7], round_send.at[stream, step])
@@ -452,13 +463,10 @@
 
 
 def fill_score(xl, expo, most, lse, targets_ref, score):
-    def step(z_at, carry):
-        factor = jnp.exp(most[xl, pl.ds(z_at, 1), :] - lse[xl, pl.ds(z_at, 1), :])
-        value = expo[xl, z_at] * factor - hit_of(targets_ref, xl, z_at).astype(F32)
-        score[0:ROWS, pl.ds(pl.multiple_of(z_at * TOK, TOK), TOK)] = value.astype(BF16)
-        return carry
-
-    lax.fori_loop(0, 8, step, 0)
+    factor = jnp.exp(most[xl] - lse[xl])
+    for z_at in range(8):
+        value = expo[xl, z_at] * factor[z_at : z_at + 1, :] - hit_of(targets_ref, xl, z_at).astype(F32)
+        score[0:ROWS, z_at * TOK : (z_at + 1) * TOK] = value.astype(BF16)
 
 
 def head_block(parts, xl, i, score):
@@ -519,8 +527,9 @@
             pltpu.VMEM((SEQ, 256), F32),
             pltpu.VMEM((2, 3, 8, TOK), F32),
             pltpu.VMEM((2, 3, 8, 8, TOK), F32),
-            pltpu.VMEM((4, SEQ, TOK), F32),
-            pltpu.VMEM((3, 8, SEQ, TOK), F32),
+            pltpu.VMEM((8, 8, TOK), F32),
+            pltpu.VMEM((3, 8, TOK), F32),
+            pltpu.VMEM((3, 8, 8, TOK), F32),
             pltpu.VMEM((256, 8 * TOK), BF16),
             dma((len(ORDER),)),
             dma((len(PHASES),)),

time: 84.5 us -> 85.7 us (1.014)
  Pallas kernels: 83.7 us -> 84.9 us
    pallas_call x1, Pallas kernels: 79.7 us -> 81.2 us  [on_device(): pl.pallas_call(main_kernel, out_shape=(pltpu.VMEM((2, 8, 8, 4, LEN_A, TOK...]
where the time goes in v7:
time: 85.7 us; the launch traced here: 85.6 us
  Pallas kernels  84.9 us (99%)
    pallas_call x1, Pallas kernels, on_device(): pl.pallas_call(main_kernel, out_shape=(pltpu.VMEM((2, 8, 8, 4, LEN_A, TOK...  81.2 us
    pallas_call x1, Pallas kernels, on_device(): pl.pallas_call(head_kernel, out_shape=(jax.ShapeDtypeStruct((1, TOK), F32...  3.75 us

profile of v7, /device:TPU:1, one launch (start us, length us, event | category | flops | bytes accessed | tf_op | source)
XLA Modules:
  0.0 85.6 jit_solution(17709141660113010810)
XLA Ops:
  0.6 81.2 %main.1 = (bf16[2,8,8,4,32,128]{5,4,3,2,1,0:T(8,128)(2,1)S(1)}, bf16[2,8,8,4,32,128]{5,4,3,2,1,0:T(8,128)(2,1)S(1)}, bf16[2,4,8,8,48,128]{5,4,3,2,1,0:T(8,128)(2...) custom-call(bf16[112,128]{1,0:T(8,128)(2,1)} %bitcast.4, ...), custom_call_target="tpu_custom_call" | custom-call | flops 5505024000 | bytes 4194304 | tf_op jit(solution)/shard_map/main/pallas_call | solution.py:504
  81.8 3.7 %head.1 = (f32[1,128]{1,0:T(1,128)}, bf16[250,3584]{1,0:T(8,128)(2,1)}) custom-call(bf16[2,8,8,4,32,128]{5,4,3,2,1,0:T(8,128)(2,1)S(1)} %get-tuple-element.13.part_a, bf16[2,8,8,4,32,128]{5,4,3,2,1,0:T(8,128)(2,1)S(1)} %get-tuple-element.14.part_b, bf16[2,4,8,8,48,128]{5,4,3,2,1,0:T(8,128)(2,1)S(1)} %get-tuple-element.15.part_c, ...), custom_call_target="tpu_custom_call" | custom-call | flops 3670016000 | bytes 2097152 | tf_op jit(solution)/shard_map/head/pallas_call | solution.py:546

commit v8 on v7

--- a/solution.py
+++ b/solution.py
@@ -21,7 +21,7 @@
 HALF = D // 2
 EXTRA = D + 128
 LEN_A, LEN_B, LEN_C = 32, 32, 48
-GROUP = 2
+GROUP = 4
 PAIR = 1
 
 
@@ -38,7 +38,7 @@
     def ring(name, unit, axis, size, length, deps, flip, hops_of=(1, 1, 1, 1)):
         far = (length // 2, length // 2 - 1)
         for step, most in zip((1, -1), far[::-1] if flip else far):
-            for dist in range(1, most + 1):
+            for dist in sorted(range(1, most + 1), key=lambda at: -hops_of[at - 1]):
                 hops = hops_of[dist - 1]
                 put((name, unit, step, dist), size, axis, hops, deps if dist == hops else [(name, unit, step, dist - hops)])
 
@@ -57,10 +57,10 @@
         2: {0: (1, -1), 1: (1, 2, 3), 3: (-1, -2, -3), 2: (2, 3, 4, 5, 6)},
         4: {0: (1, 2, 3, -1, -2, -3), 1: tuple(range(1, 8))},
     }
-    direct("CQ", "q", LEN_C, (1, -1, 2, -2, 3, -3, 4))
-    direct("XA", "x", LEN_A, (1, -1, 2))
-    direct("XB", "x", LEN_B, (1, -1, 2))
-    ring("CP", 0, "p", 8 * LEN_C, 8, of("CQ"), False, (1, 2, 1, 1))
+    direct("CQ", "q", LEN_C, (4, 3, -3, 2, -2, 1, -1))
+    direct("XA", "x", LEN_A, (2, 1, -1))
+    direct("XB", "x", LEN_B, (2, 1, -1))
+    ring("CP", 0, "p", 8 * LEN_C, 8, of("CQ"), False)
     for unit, rels in whole[PAIR].items():
         deps = of("CQ") + [key for rel in rels for key in item("CP", rel, False)]
         ring("CX", unit, "x", PAIR * 8 * LEN_C, 4, deps, unit % 2 == 1)
@@ -99,7 +99,7 @@
 
     def start(core, key, now):
         m = messages[key]
-        free[core] = now = max(now, free[core]) + 0.1
+        free[core] = now = max(now, free[core]) + 0.05
         lane = ("s", core) if m["axis"] == "s" else (turned[m["axis"]] if core else m["axis"], key[2])
         rate = 6e5 if m["axis"] == "s" else 8.5e4
         link[lane] = max(now, link.get(lane, 0.0)) + m["size"] * m["hops"] / rate
@@ -168,8 +168,9 @@
         x_at = lax.div(other, 2)
         return (lax.div(x_at, 2) * 16 + y * 2 + lax.rem(other, 2), lax.rem(x_at, 2) * 8 + z)
 
-    x_peers, y_peers, z_peers = ([peer(r) for r in range(1, 8)] for peer in (x_peer, y_peer, z_peer))
-    z_places = [lax.rem(z + r, 8) for r in range(1, 8)]
+    far_first = (4, 3, 5, 2, 6, 1, 7)
+    x_peers, y_peers, z_peers = ([peer(r) for r in far_first] for peer in (x_peer, y_peer, z_peer))
+    z_places = [lax.rem(z + r, 8) for r in far_first]
     sibling = (v + 1 - 2 * c, s)
     a, b, cc = part_a.at[c], part_b.at[c], part_c.at[c]
 
@@ -182,18 +183,14 @@
     grad_copy = pltpu.make_async_copy(input_grad_ref, grad_v, local_sem.at[4])
     targets_copy = pltpu.make_async_copy(targets_hbm, targets_ref, local_sem.at[5])
     table_copy = pltpu.make_async_copy(table_ref, table_v, local_sem.at[6])
-    for copy in own:
-        copy.start()
-    table_copy.start()
-
-    partners = [device(turn(x, d, 4), p, q) for d in (1, -1, 2)]
-    partners += [device(x, turn(p, d, 8), q) for d in (1, -1, 2, -2)]
-    partners += [device(x, p, turn(q, d, 8)) for d in (1, -1, 2, -2, 3, -3, 4)]
+    partners = [device(x, p, turn(q, d, 8)) for d in (4, 3, -3, 2, -2, 1, -1)]
+    partners += [device(x, turn(p, d, 8), q) for d in (2, -2, 1, -1)]
+    partners += [device(turn(x, d, 4), p, q) for d in (2, 1, -1)]
     partners += [sibling]
     barrier = pltpu.get_barrier_semaphore()
     for partner in partners:
         pl.semaphore_signal(barrier, inc=1, device_id=partner, device_id_type=MESH)
-    for copy in (ids_copy, grad_copy, targets_copy):
+    for copy in own + [table_copy, ids_copy, grad_copy, targets_copy]:
         copy.start()
 
     def split_columns(core, j):
@@ -402,18 +399,18 @@
     statistics_step(jnp.int32(7))
     send_round(1, 0)
     send_round(2, 0)
-    for step in range(2):
-        for stream in range(3):
-            data, _ = round_refs(stream, step + 1)
-            data[...] = merged(stream, step)
-            send_round(stream, step + 1)
+
+    def next_round(stream, step):
+        data, _ = round_refs(stream, step + 1)
+        data[...] = merged(stream, step)
+        send_round(stream, step + 1)
+
+    for stream, step in ((0, 0), (1, 0), (2, 0), (0, 1), (1, 1)):
+        next_round(stream, step)
+
     embed_arrived()
-
     hot = emb_hot[...].astype(BF16)
     hot = jnp.concatenate([hot, hot, hot], axis=0)
-    lse[0] = merged(0, 2)
-    fill_score(0, expo, most, lse, targets_ref, score)
-
     for i in range(4):
         rest = emb_rows[:, i * (D // 4) : (i + 1) * (D // 4)]
         high = rest.astype(BF16)
@@ -421,8 +418,13 @@
         middle = rest.astype(BF16)
         low = (rest - middle.astype(F32)).astype(BF16)
         terms = jnp.concatenate([high, middle, low], axis=0)
-        embed = lax.dot_general(terms, hot, (((0,), (0,)), ((), ())), preferred_element_type=F32)
-        turned[i] = head_block(parts, 0, i, score) + embed
+        turned[i] = lax.dot_general(terms, hot, (((0,), (0,)), ((), ())), preferred_element_type=F32)
+
+    next_round(2, 1)
+    lse[0] = merged(0, 2)
+    fill_score(0, expo, most, lse, targets_ref, score)
+    for i in range(4):
+        turned[i] += head_block(parts, 0, i, score)
     lse[1] = merged(1, 2)
     pick_out[0] = merged(2, 2)
     loss_ref[...] = lse[xl_here, pl.ds(z, 1), :] - pick_out[0, pl.ds(xl_here, 1), :]

time: 85.7 us -> 83.4 us (0.973)
  Pallas kernels: 84.9 us -> 82.6 us
    pallas_call x1, Pallas kernels: 81.2 us -> 78.9 us  [on_device(): pl.pallas_call(main_kernel, out_shape=(pltpu.VMEM((2, 8, 8, 4, LEN_A, TOK...]
where the time goes in v8:
time: 83.4 us; the launch traced here: 83.3 us
  Pallas kernels  82.6 us (99%)
    pallas_call x1, Pallas kernels, on_device(): pl.pallas_call(main_kernel, out_shape=(pltpu.VMEM((2, 8, 8, 4, LEN_A, TOK...  78.9 us
    pallas_call x1, Pallas kernels, on_device(): pl.pallas_call(head_kernel, out_shape=(jax.ShapeDtypeStruct((1, TOK), F32...  3.75 us

profile of v8, /device:TPU:1, one launch (start us, length us, event | category | flops | bytes accessed | tf_op | source)
XLA Modules:
  0.0 83.3 jit_solution(18143459137752475968)
XLA Ops:
  0.6 78.9 %main.1 = (bf16[2,8,8,4,32,128]{5,4,3,2,1,0:T(8,128)(2,1)S(1)}, bf16[2,8,8,4,32,128]{5,4,3,2,1,0:T(8,128)(2,1)S(1)}, bf16[2,4,8,8,48,128]{5,4,3,2,1,0:T(8,128)(2...) custom-call(bf16[112,128]{1,0:T(8,128)(2,1)} %bitcast.4, ...), custom_call_target="tpu_custom_call" | custom-call | flops 5505024000 | bytes 4194304 | tf_op jit(solution)/shard_map/main/pallas_call | solution.py:506
  79.5 3.7 %head.1 = (f32[1,128]{1,0:T(1,128)}, bf16[250,3584]{1,0:T(8,128)(2,1)}) custom-call(bf16[2,8,8,4,32,128]{5,4,3,2,1,0:T(8,128)(2,1)S(1)} %get-tuple-element.13.part_a, bf16[2,8,8,4,32,128]{5,4,3,2,1,0:T(8,128)(2,1)S(1)} %get-tuple-element.14.part_b, bf16[2,4,8,8,48,128]{5,4,3,2,1,0:T(8,128)(2,1)S(1)} %get-tuple-element.15.part_c, ...), custom_call_target="tpu_custom_call" | custom-call | flops 3670016000 | bytes 2097152 | tf_op jit(solution)/shard_map/head/pallas_call | solution.py:548

commit v9 on v8

--- a/solution.py
+++ b/solution.py
@@ -72,7 +72,6 @@
             ring(name, unit, axis, 4 * GROUP * size, 8, deps, unit % 2 == 1)
     put(("SA", 0, 0, 0), 32 * LEN_A, "s", 1, of("XA", "AQ"))
     put(("SB", 0, 0, 0), 32 * LEN_B, "s", 1, of("XB", "BP"))
-    put(("SC", 0, 0, 0), 64 * LEN_C, "s", 1, of("CQ", "CP"))
     for rel in range(1, 8):
         for name, source, size in (("SA", "AP", LEN_A), ("SB", "BQ", LEN_B)):
             keys = [key for key in of(source) if (-key[2] * key[3]) % 8 == rel]
@@ -81,8 +80,13 @@
                     put((name,) + key, messages[key]["size"] // 256, "s", 1, [key])
             else:
                 put((name, rel, 0, 0), 32 * size, "s", 1, keys)
-    for key in of("CX"):
-        put(("SC",) + key, PAIR * 8 * LEN_C, "s", 1, [key])
+    for rel in range(8):
+        keys = [key for key in of("CP") if (-key[2] * key[3]) % 8 == rel] + [key for key in of("CX") if key[1] == rel]
+        if rel == 4:
+            for key in keys:
+                put(("SC",) + key, messages[key]["size"] // 256, "s", 1, [key])
+        else:
+            put(("SC", rel, 0, 0), 32 * LEN_C, "s", 1, of("CQ") + keys)
     return messages
 
 
@@ -206,7 +210,7 @@
 
     splits = [(core, j) for core in range(2) for j in range(HALF // 256)]
     table_copy.wait()
-    for core, j in splits[:8]:
+    for core, j in splits[:5]:
         split_columns(core, j)
     for copy in own:
         copy.wait()
@@ -241,7 +245,7 @@
             return a.at[turn(p, unit, 8)]
         if name == "SB":
             return b.at[turn(q, unit, 8)]
-        return cc.at[x]
+        return cc.at[:, turn(p, unit, 8)]
 
     def arrived(key):
         return block(key, -key[2] * key[3])
@@ -302,7 +306,7 @@
 
     needed = {key for key in MESSAGES if key[0] in ("XA", "XB", "AQ", "BP")}
     middle = max(36, 1 + max(ORDER.index(key) for key in needed))
-    others = [functools.partial(split_columns, *split) for split in splits[8:]]
+    others = [functools.partial(split_columns, *split) for split in splits[5:]]
     others += [embed_rows] + [functools.partial(send_row, r) for r in range(1, SEQ)]
     send_ready()
     for i, key in enumerate(ORDER):

time: 83.4 us -> 83.4 us (level)
  no operation moved by 1% of the time
where the time goes in v9:
time: 83.4 us; the launch traced here: 83.3 us
  Pallas kernels  82.7 us (99%)
    pallas_call x1, Pallas kernels, on_device(): pl.pallas_call(main_kernel, out_shape=(pltpu.VMEM((2, 8, 8, 4, LEN_A, TOK...  78.9 us
    pallas_call x1, Pallas kernels, on_device(): pl.pallas_call(head_kernel, out_shape=(jax.ShapeDtypeStruct((1, TOK), F32...  3.75 us

profile of v9, /device:TPU:1, one launch (start us, length us, event | category | flops | bytes accessed | tf_op | source)
XLA Modules:
  0.0 83.3 jit_solution(10097300526418151260)
XLA Ops:
  0.6 78.9 %main.1 = (bf16[2,8,8,4,32,128]{5,4,3,2,1,0:T(8,128)(2,1)S(1)}, bf16[2,8,8,4,32,128]{5,4,3,2,1,0:T(8,128)(2,1)S(1)}, bf16[2,4,8,8,48,128]{5,4,3,2,1,0:T(8,128)(2...) custom-call(bf16[112,128]{1,0:T(8,128)(2,1)} %bitcast.4, ...), custom_call_target="tpu_custom_call" | custom-call | flops 5505024000 | bytes 4194304 | tf_op jit(solution)/shard_map/main/pallas_call | solution.py:510
  79.5 3.7 %head.1 = (f32[1,128]{1,0:T(1,128)}, bf16[250,3584]{1,0:T(8,128)(2,1)}) custom-call(bf16[2,8,8,4,32,128]{5,4,3,2,1,0:T(8,128)(2,1)S(1)} %get-tuple-element.13.part_a, bf16[2,8,8,4,32,128]{5,4,3,2,1,0:T(8,128)(2,1)S(1)} %get-tuple-element.14.part_b, bf16[2,4,8,8,48,128]{5,4,3,2,1,0:T(8,128)(2,1)S(1)} %get-tuple-element.15.part_c, ...), custom_call_target="tpu_custom_call" | custom-call | flops 3670016000 | bytes 2097152 | tf_op jit(solution)/shard_map/head/pallas_call | solution.py:552

commit v10 on v9

--- a/solution.py
+++ b/solution.py
@@ -127,6 +127,7 @@
 MESSAGES = plan_messages()
 ORDER = plan_order(MESSAGES)
 RECV = {key: i for i, key in enumerate(ORDER)}
+OWN_ROWS = {"XA": pl.ds(0, LEN_A), "XB": pl.ds(LEN_A, LEN_B), "CQ": pl.ds(LEN_A + LEN_B, LEN_C)}
 PHASES = ("XA", "XB", "CQ", "CP", "CX", "AQ", "BP", "AP", "BQ")
 
 
@@ -209,11 +210,6 @@
         table_c[core, :, n0 : n0 + 256] = columns.astype(BF16)
 
     splits = [(core, j) for core in range(2) for j in range(HALF // 256)]
-    table_copy.wait()
-    for core, j in splits[:5]:
-        split_columns(core, j)
-    for copy in own:
-        copy.wait()
     pl.semaphore_wait(barrier, len(partners))
 
     def group(at, unit, size):
@@ -264,8 +260,9 @@
                 "q": lambda: device(x, p, turn(q, by, 8)),
             }[m["axis"]]()
             sems = send_sem.at[PHASES.index(key[0])], recv_sem.at[RECV[key]]
+        source = hidden_ref.at[OWN_ROWS[key[0]]] if key[0] in OWN_ROWS else data
         pltpu.make_async_remote_copy(
-            src_ref=data, dst_ref=data, send_sem=sems[0], recv_sem=sems[1], device_id=target, device_id_type=MESH
+            src_ref=source, dst_ref=data, send_sem=sems[0], recv_sem=sems[1], device_id=target, device_id_type=MESH
         ).start()
 
     done, sent = set(), set()
@@ -306,9 +303,14 @@
 
     needed = {key for key in MESSAGES if key[0] in ("XA", "XB", "AQ", "BP")}
     middle = max(36, 1 + max(ORDER.index(key) for key in needed))
-    others = [functools.partial(split_columns, *split) for split in splits[5:]]
+    others = [functools.partial(split_columns, *split) for split in splits[9:]]
     others += [embed_rows] + [functools.partial(send_row, r) for r in range(1, SEQ)]
     send_ready()
+    table_copy.wait()
+    for core, j in splits[:9]:
+        split_columns(core, j)
+    for copy in own:
+        copy.wait()
     for i, key in enumerate(ORDER):
         wait_bytes(arrived(key), recv_sem.at[RECV[key]])
         done.add(key)

time: 83.4 us -> 84.2 us (level)
  no operation moved by 1% of the time
where the time goes in v10:
time: 84.2 us; the launch traced here: 84 us
  Pallas kernels  83.4 us (99%)
    pallas_call x1, Pallas kernels, on_device(): pl.pallas_call(main_kernel, out_shape=(pltpu.VMEM((2, 8, 8, 4, LEN_A, TOK...  79.7 us
    pallas_call x1, Pallas kernels, on_device(): pl.pallas_call(head_kernel, out_shape=(jax.ShapeDtypeStruct((1, TOK), F32...  3.75 us

profile of v10, /device:TPU:1, one launch (start us, length us, event | category | flops | bytes accessed | tf_op | source)
XLA Modules:
  0.0 84.0 jit_solution(9735231355488671371)
XLA Ops:
  0.6 79.7 %main.1 = (bf16[2,8,8,4,32,128]{5,4,3,2,1,0:T(8,128)(2,1)S(1)}, bf16[2,8,8,4,32,128]{5,4,3,2,1,0:T(8,128)(2,1)S(1)}, bf16[2,4,8,8,48,128]{5,4,3,2,1,0:T(8,128)(2...) custom-call(bf16[112,128]{1,0:T(8,128)(2,1)} %bitcast.4, ...), custom_call_target="tpu_custom_call" | custom-call | flops 5505024000 | bytes 4194304 | tf_op jit(solution)/shard_map/main/pallas_call | solution.py:512
  80.3 3.7 %head.1 = (f32[1,128]{1,0:T(1,128)}, bf16[250,3584]{1,0:T(8,128)(2,1)}) custom-call(bf16[2,8,8,4,32,128]{5,4,3,2,1,0:T(8,128)(2,1)S(1)} %get-tuple-element.13.part_a, bf16[2,8,8,4,32,128]{5,4,3,2,1,0:T(8,128)(2,1)S(1)} %get-tuple-element.14.part_b, bf16[2,4,8,8,48,128]{5,4,3,2,1,0:T(8,128)(2,1)S(1)} %get-tuple-element.15.part_c, ...), custom_call_target="tpu_custom_call" | custom-call | flops 3670016000 | bytes 2097152 | tf_op jit(solution)/shard_map/head/pallas_call | solution.py:554
